TPU v7x, 256 devices: a whole 4x4x8 slice. The times are simulated.
256 devices in a mesh: blk: 8 (over y, x_lo), dp: 32 (over x_hi, z, core).
Axes of the slice: x: 4 (x_hi: 2, x_lo: 2; x = x_hi * 2 + x_lo), y: 4, z: 8, core: 2. Of those that a mesh axis runs over, the one named last changes fastest.
Arguments:
- image_feats: bfloat16 [131072, 1152], P(('blk', 'dp')), may hold values from -24 to 24
- text_feats: bfloat16 [131072, 1152], P(('blk', 'dp')), may hold values from -24 to 24
- image_head: bfloat16 [1152, 1152], replicated, may hold values from -0.1875 to 0.1875
- text_head: bfloat16 [1152, 1152], replicated, may hold values from -0.1875 to 0.1875
Outputs:
- row_loss: float32 [131072], P(('blk', 'dp'))
- image_head_grad: float32 [1152, 1152], P('dp', 'blk')
- text_head_grad: float32 [1152, 1152], P('dp', 'blk')
All inputs are finite; a program needn't handle non-finite values.
Results may differ from a plain program's by a relative error of at most 0.0026.
Values may be sent and summed in bfloat16 or wider, within the bound.
No kernel may reach another device: no remote copies, remote signals or barrier semaphores. Data moves between devices by JAX's collectives and lax.ppermute only.
A program may use at most 128 MiB of HBM per device.

v0:
```python
import jax
import jax.numpy as jnp
from jax import lax
from jax.sharding import PartitionSpec as P

TEMP = 30.0
BIAS = -6.0
EPS = 1e-06


def shifted(value, axis, steps):
    count = lax.axis_size(axis)
    pairs = [(source, (source + steps) % count) for source in range(count)]
    return lax.ppermute(value, axis, pairs)


def embed(feats, head):
    proj = jnp.dot(feats, head, preferred_element_type=jnp.float32)
    norm = jnp.sqrt(jnp.sum(proj * proj, axis=1, keepdims=True) + EPS)
    return (proj / norm, norm)


def pair_terms(image_emb, text_emb, diagonal):
    logits = TEMP * jnp.dot(image_emb, text_emb.T, preferred_element_type=jnp.float32) + BIAS
    count = logits.shape[0]
    if diagonal:
        eye = lax.broadcasted_iota(jnp.int32, (count, count), 0) == lax.broadcasted_iota(
            jnp.int32, (count, count), 1
        )
        labels = jnp.where(eye, 1.0, -1.0).astype(jnp.float32)
    else:
        labels = -jnp.ones((count, count), jnp.float32)
    loss = jnp.sum(-jax.nn.log_sigmoid(labels * logits), axis=1)
    weights = (-labels * jax.nn.sigmoid(-labels * logits) / count).astype(jnp.bfloat16)
    image_grad = TEMP * jnp.dot(weights, text_emb, preferred_element_type=jnp.float32)
    text_grad = TEMP * lax.dot_general(
        weights, image_emb, (((0,), (0,)), ((), ())), preferred_element_type=jnp.float32
    )
    return (loss, image_grad, text_grad)


def head_back(feats, unit, norm, emb_grad):
    proj_grad = ((emb_grad - unit * jnp.sum(unit * emb_grad, axis=1, keepdims=True)) / norm).astype(
        jnp.bfloat16
    )
    return lax.dot_general(
        feats, proj_grad, (((0,), (0,)), ((), ())), preferred_element_type=jnp.float32
    )


def advance_text(visiting):
    return shifted(visiting, "blk", 1)


def body(image_feats, text_feats, image_head, text_head):
    image_unit, image_norm = embed(image_feats, image_head)
    text_unit, text_norm = embed(text_feats, text_head)
    image_emb = image_unit.astype(jnp.bfloat16)
    text_emb = text_unit.astype(jnp.bfloat16)
    row_loss, image_grad, text_accum = pair_terms(image_emb, text_emb, True)
    visiting = text_emb
    for step in range(2):
        visiting = advance_text(visiting)
        text_accum = shifted(text_accum, "blk", 1)
        loss, igrad, tgrad = pair_terms(image_emb, visiting, False)
        row_loss = row_loss + loss
        image_grad = image_grad + igrad
        text_accum = text_accum + tgrad
    text_grad = shifted(text_accum, "blk", -2)
    image_terms = head_back(image_feats, image_unit, image_norm, image_grad)
    text_terms = head_back(text_feats, text_unit, text_norm, text_grad)
    image_part, text_part = (
        lax.psum_scatter(image_terms, "blk", scatter_dimension=1, tiled=True),
        lax.psum_scatter(text_terms, "blk", scatter_dimension=1, tiled=True),
    )
    image_head_grad, text_head_grad = (
        lax.psum_scatter(image_part, "dp", scatter_dimension=0, tiled=True),
        lax.psum_scatter(text_part, "dp", scatter_dimension=0, tiled=True),
    )
    return (row_loss, image_head_grad, text_head_grad)


def solution(mesh):
    placed = (P(("blk", "dp"), None), P(("blk", "dp"), None), P(), P())
    return jax.shard_map(
        body,
        mesh=mesh,
        in_specs=placed,
        out_specs=(P(("blk", "dp")), P("dp", "blk"), P("dp", "blk")),
        check_vma=False,
    )
```

profile of v0, /device:TPU:10, one launch (start us, length us, event | category | flops | bytes accessed | tf_op | source)
XLA Modules:
  0.0 725.2 jit_solution(9413785445132050091)
XLA Ops:
  7.2 1.7 copy-done
  8.9 3.3 multiply_reduce_fusion.2
  12.5 1.6 collective-permute-start
  14.8 1.9 multiply_reduce_fusion.3
  17.0 23.2 %collective-permute-done = bf16[512,1152]{1,0:T(8,128)(2,1)S(1)} collective-permute-done((bf16[512,1152]{1,0:T(8,128)(2,1)S(1)}, bf16[512,1152]{1,0:T(8,128)(2,1)S(1)}, u32[]{:S(2)}, u32[]{:S(2)}) %collective-permute-start) | collective-permute-done | bytes 1179680 | tf_op jit(solution)/shard_map/ppermute | solution.py:14
  40.3 2.4 collective-permute-start.1
  42.7 1.4 fusion.16
  45.2 1.4 fusion.17
  47.6 19.5 %collective-permute-done.1 = bf16[512,1152]{1,0:T(8,128)(2,1)S(1)} collective-permute-done((bf16[512,1152]{1,0:T(8,128)(2,1)S(1)}, bf16[512,1152]{1,0:T(8,128)(2,1)S(1)}, u32[]{:S(2)}, u32[]{:S(2)}) %collective-permute-start.1) | collective-permute-done | bytes 1179680 | tf_op jit(solution)/shard_map/ppermute | solution.py:14
  67.1 1.4 fusion.18
  68.5 1.3 multiply_reduce_fusion.1
  69.8 4.4 convolution_bitcast_fusion.1
  74.3 2.7 convolution_multiply_fusion.2
  77.0 3.4 collective-permute-start.2
  80.4 91.9 %collective-permute-done.2 = f32[512,1152]{1,0:T(8,128)S(1)} collective-permute-done((f32[512,1152]{1,0:T(8,128)S(1)}, f32[512,1152]{1,0:T(8,128)S(1)}, u32[]{:S(2)}, u32[]{:S(2)}) %collective-permute-start.2) | collective-permute-done | bytes 2359328 | tf_op jit(solution)/shard_map/ppermute | solution.py:14
  172.3 1.0 fusion.1
  173.3 3.7 collective-permute-start.3
  177.0 1.0 convolution_multiply_fusion
  178.0 98.2 %collective-permute-done.3 = f32[512,1152]{1,0:T(8,128)S(1)} collective-permute-done((f32[512,1152]{1,0:T(8,128)S(1)}, f32[512,1152]{1,0:T(8,128)S(1)}, u32[]{:S(2)}, u32[]{:S(2)}) %collective-permute-start.3) | collective-permute-done | bytes 2359328 | tf_op jit(solution)/shard_map/ppermute | solution.py:14
  276.8 47.8 %collective-permute-done.4 = f32[512,1152]{1,0:T(8,128)S(1)} collective-permute-done((f32[512,1152]{1,0:T(8,128)S(1)}, f32[512,1152]{1,0:T(8,128)S(1)}, u32[]{:S(2)}, u32[]{:S(2)}) %collective-permute-start.4) | collective-permute-done | bytes 2359328 | tf_op jit(solution)/shard_map/ppermute | solution.py:14
  325.0 4.3 convolution_bitcast_fusion
  329.4 119.7 %reduce-scatter.7.cloned.1.call-done = f32[1152,144]{0,1:T(8,128)} async-done(((f32[1152,1152]{0,1:T(8,128)}), f32[1152,144]{0,1:T(8,128)}) %reduce-scatter.7.cloned.1.call-update) | async-done | bytes 663568 | tf_op jit(solution)/shard_map/reduce_scatter | solution.py:74
  451.0 265.2 %all-reduce.5.cloned.1.call-done = (f32[1152,144]{0,1:T(8,128)}, f32[1152,144]{0,1:T(8,128)}) async-done(((f32[1152,144]{0,1:T(8,128)}, f32[1152,144]{0,1:T(8,128)}), (f32[1152,144]{0,1:T(8,128)}, f32[1152,144]{0,1:T(8,128)})) %all-reduce.5.cloned.1.call-update) | async-done | bytes 1327120
  716.2 1.1 constant_dynamic-slice_fusion
  (47 shorter events, 7.1 us)
Async XLA Ops:
  7.2 1.8 copy-start
  7.2 322.2 %reduce-scatter.5.cloned.1.call-start = ((), (), s32[]{:S(2)}) async-start(), calls=%async_computation.2 | async-start | bytes 5971968 | tf_op jit(solution)/shard_map/reduce_scatter | solution.py:73
  8.9 5.2 copy-start.6
  12.2 4.5 copy-start.1
  12.2 2.6 copy-start.5
  12.5 27.8 %collective-permute-start = (bf16[512,1152]{1,0:T(8,128)(2,1)S(1)}, bf16[512,1152]{1,0:T(8,128)(2,1)S(1)}, u32[]{:S(2)}, u32[]{:S(2)}) collective-permute-start(bf16[512,1152]{1,0:T(8,128)(2,1)S(1)} %fusion.21), channel_id=1, source_target_pairs={{0,32},{32,64},{64,96},{96,128},{128,160},{160,192},{192,224},{224... | collective-permute-start | bytes 3538952 | tf_op jit(solution)/shard_map/ppermute | solution.py:14
  17.0 50.1 %copy-start.3 = (bf16[512,1152]{1,0:T(8,128)(2,1)}, bf16[512,1152]{1,0:T(8,128)(2,1)S(1)}, u32[]{:S(2)}) copy-start(bf16[512,1152]{1,0:T(8,128)(2,1)S(1)} %fusion.20) | copy-start | bytes 3538948
  40.3 26.8 %collective-permute-start.1 = (bf16[512,1152]{1,0:T(8,128)(2,1)S(1)}, bf16[512,1152]{1,0:T(8,128)(2,1)S(1)}, u32[]{:S(2)}, u32[]{:S(2)}) collective-permute-start(bf16[512,1152]{1,0:T(8,128)(2,1)S(1)} %collective-permute-done), channel_id=1, source_target_pairs={{0,32},{32,64},{64,96},{96,128},{128,160},{160,192},{192,224},{224... | collective-permute-start | bytes 3538952 | tf_op jit(solution)/shard_map/ppermute | solution.py:14
  44.2 1.0 copy-start.13
  46.6 1.0 copy-start.9
  68.5 1.3 copy-start.11
  74.2 375.0 %reduce-scatter.7.cloned.1.call-start = ((), (), s32[]{:S(2)}) async-start(), calls=%async_computation.3 | async-start | bytes 5971968 | tf_op jit(solution)/shard_map/reduce_scatter | solution.py:74
  74.2 98.1 %copy-start.4 = (bf16[512,1152]{1,0:T(8,128)(2,1)S(1)}, bf16[512,1152]{1,0:T(8,128)(2,1)}, u32[]{:S(2)}) copy-start(bf16[512,1152]{1,0:T(8,128)(2,1)} %copy-done.3) | copy-start | bytes 3538948
  74.2 98.1 %copy-start.10 = (f32[512,512]{0,1:T(8,128)S(1)}, f32[512,512]{0,1:T(8,128)}, u32[]{:S(2)}) copy-start(f32[512,512]{0,1:T(8,128)} %copy-done.9) | copy-start | bytes 3145732
  77.0 100.0 %copy-start.12 = (f32[512,512]{0,1:T(8,128)S(1)}, f32[512,512]{0,1:T(8,128)}, u32[]{:S(2)}) copy-start(f32[512,512]{0,1:T(8,128)} %copy-done.11) | copy-start | bytes 3145732
  77.0 95.3 %collective-permute-start.2 = (f32[512,1152]{1,0:T(8,128)S(1)}, f32[512,1152]{1,0:T(8,128)S(1)}, u32[]{:S(2)}, u32[]{:S(2)}) collective-permute-start(f32[512,1152]{1,0:T(8,128)S(1)} %convolution_multiply_fusion.2), channel_id=1, source_target_pairs={{0,32},{32,64},{64,96},{96,128},{128,160},{160,192},{192,224},{224... | collective-permute-start | bytes 7077896 | tf_op jit(solution)/shard_map/ppermute | solution.py:14
  173.3 102.8 %collective-permute-start.3 = (f32[512,1152]{1,0:T(8,128)S(1)}, f32[512,1152]{1,0:T(8,128)S(1)}, u32[]{:S(2)}, u32[]{:S(2)}) collective-permute-start(f32[512,1152]{1,0:T(8,128)S(1)} %fusion.1), channel_id=1, source_target_pairs={{0,32},{32,64},{64,96},{96,128},{128,160},{160,192},{192,224},{224... | collective-permute-start | bytes 7077896 | tf_op jit(solution)/shard_map/ppermute | solution.py:14
  178.0 146.7 %copy-start.2 = (f32[512,1152]{1,0:T(8,128)S(1)}, f32[512,1152]{1,0:T(8,128)}, u32[]{:S(2)}) copy-start(f32[512,1152]{1,0:T(8,128)} %copy-done.1) | copy-start | bytes 7077892
  276.4 48.6 %copy-start.7 = (bf16[512,1152]{1,0:T(8,128)(2,1)S(1)}, bf16[512,1152]{1,0:T(8,128)(2,1)}, u32[]{:S(2)}) copy-start(bf16[512,1152]{1,0:T(8,128)(2,1)} %param.5) | copy-start | bytes 3538948
  276.4 48.2 %collective-permute-start.4 = (f32[512,1152]{1,0:T(8,128)S(1)}, f32[512,1152]{1,0:T(8,128)S(1)}, u32[]{:S(2)}, u32[]{:S(2)}) collective-permute-start(f32[512,1152]{1,0:T(8,128)S(1)} %add.87), channel_id=1, source_target_pairs={{0,192},{32,224},{64,0},{96,32},{128,64},{160,96},{192,128},{224,1... | collective-permute-start | bytes 7077896 | tf_op jit(solution)/shard_map/ppermute | solution.py:14
  329.3 119.9 %copy-start.8 = (u32[256]{0:T(256)S(1)}, u32[256]{0:T(256)}, u32[]{:S(2)}) copy-start(u32[256]{0:T(256)} %constant.27) | copy-start | bytes 3076
  329.3 386.9 %all-reduce.5.cloned.1.call-start = ((), (), s32[]{:S(2)}) async-start(), calls=%async_computation.4 | async-start | bytes 2654208
Sparse Core Ops, SparseCore 0:
  74.3 206.9 reduce-scatter.4
  329.5 119.6 reduce-scatter.6
  451.9 264.2 all-reduce.4
where the time goes:
time: 726 us; the launch traced here: 725 us
  waiting for transfers between devices  666 us (92%)
  matrix products  26 us (4%)
  between operations  14.6 us (2%)
  starting transfers between devices  11.7 us (2%)
    ppermute x5, waiting for transfers between devices, shifted(): return lax.ppermute(value, axis, pairs)  281 us
    unnamed x4, waiting for transfers between devices  265 us
    reduce_scatter x1, waiting for transfers between devices, body(): lax.psum_scatter(text_terms, 'blk', scatter_dimension=1, tiled=True)  120 us
  transfers between devices with their start and end apart: 8, of which 7 were waited for; matrix products, arithmetic and copies ran while one was open for 2% of the time, Pallas kernels for 0%

commit v1 on v0

v1 whole, which is shorter than its diff:
```python
import jax
import jax.numpy as jnp
from jax import lax
from jax.sharding import PartitionSpec as P

TEMP = 30.0
BIAS = -6.0
EPS = 1e-06
F32 = jnp.float32
BF16 = jnp.bfloat16


def embed(feats, head):
    proj = jnp.dot(feats, head, preferred_element_type=F32)
    norm = jnp.sqrt(jnp.sum(proj * proj, axis=1, keepdims=True) + EPS)
    return (proj / norm, norm)


def blk_move(value, even, odd):
    count = lax.axis_size("blk")
    pairs = [(k, (even(k) if k % 2 == 0 else odd(k)) % count) for k in range(count)]
    return lax.ppermute(value, "blk", pairs)


def other_core(value):
    count = lax.axis_size("dp")
    return lax.ppermute(value, "dp", [(k, k ^ 1) for k in range(count)])


def pair_weights(mine, theirs, diagonal):
    logits = TEMP * lax.dot_general(mine, theirs, (((1,), (1,)), ((), ())), preferred_element_type=F32) + BIAS
    count = logits.shape[0]
    if diagonal:
        eye = lax.broadcasted_iota(jnp.int32, logits.shape, 0) == lax.broadcasted_iota(jnp.int32, logits.shape, 1)
        labels = jnp.where(eye, 1.0, -1.0).astype(F32)
    else:
        labels = -jnp.ones(logits.shape, F32)
    loss = jnp.sum(-jax.nn.log_sigmoid(labels * logits), axis=1)
    weights = (-labels * jax.nn.sigmoid(-labels * logits) / count).astype(BF16)
    return loss, weights


def side(mine, partners):
    loss, grad = 0.0, 0.0
    for step, theirs in enumerate(partners):
        part, weights = pair_weights(mine, theirs, step == 0)
        loss = loss + part
        grad = grad + jnp.dot(weights, theirs, preferred_element_type=F32)
    return loss, TEMP * grad


def proj_grad(unit, norm, grad):
    return ((grad - unit * jnp.sum(unit * grad, axis=1, keepdims=True)) / norm).astype(BF16)


def row_dot(left, right):
    return lax.dot_general(left, right, (((0,), (0,)), ((), ())), preferred_element_type=F32)


def core_columns(feats, core):
    d = feats.shape[1]
    row = lax.broadcasted_iota(jnp.int32, (d, d // 2), 0)
    col = lax.broadcasted_iota(jnp.int32, (d, d // 2), 1)
    chosen = row == (col // 36) * 72 + core * 36 + col % 36
    return jnp.dot(feats, chosen.astype(BF16), preferred_element_type=F32).astype(BF16)


def body(image_feats, text_feats, image_head, text_head):
    even = lax.axis_index("blk") % 2 == 0
    core = lax.axis_index("dp") % 2
    image_unit, image_norm = embed(image_feats, image_head)
    text_unit, text_norm = embed(text_feats, text_head)

    def pick(x, y):
        return jnp.where(even, x, y)

    a_unit, b_unit = pick(text_unit, image_unit), pick(image_unit, text_unit)
    a_norm, b_norm = pick(text_norm, image_norm), pick(image_norm, text_norm)
    a_emb, b_emb = a_unit.astype(BF16), b_unit.astype(BF16)

    swap = (lambda k: k + 1, lambda k: k - 1)
    b_from = blk_move(b_emb, lambda k: k - 2, lambda k: k + 2)
    a_cross = blk_move(a_emb, *swap)
    a_from = blk_move(a_emb, lambda k: k + 2, lambda k: k - 2)
    b_cross = blk_move(b_from, *swap)

    a_feats = pick(text_feats, image_feats)
    b_feats = pick(image_feats, text_feats)
    a_own, b_own = core_columns(a_feats, core), core_columns(b_feats, core)
    a_oth = other_core(core_columns(a_feats, 1 - core))
    b_oth = other_core(core_columns(b_feats, 1 - core))

    def head_terms(unit, norm, grad, own, oth):
        mine = proj_grad(unit, norm, grad)
        theirs = other_core(mine)
        terms = (row_dot(mine, own) + row_dot(theirs, oth)).astype(BF16)
        terms = terms.reshape(8, 144, 576)
        return lax.all_to_all(terms, "blk", 0, 0)

    a_loss, a_grad = side(a_emb, (b_emb, a_cross, b_from))
    a_got = head_terms(a_unit, a_norm, a_grad, a_own, a_oth)
    b_loss, b_grad = side(b_emb, (a_emb, b_cross, a_from))
    b_got = head_terms(b_unit, b_norm, b_grad, b_own, b_oth)

    a_got = a_got.reshape(4, 2, 144, 576).astype(F32).sum(0)
    b_got = b_got.reshape(4, 2, 144, 576).astype(F32).sum(0)
    both = jnp.stack([a_got[1] + b_got[0], a_got[0] + b_got[1]])
    both = both.reshape(2, 144, 16, 36).transpose(2, 3, 0, 1).reshape(16, 36, 288)
    groups = [[2 * j + c for j in range(16)] for c in range(2)]
    both = lax.all_to_all(both, "dp", 0, 0, axis_index_groups=groups).sum(0)
    row_loss = pick(b_loss, a_loss)
    return row_loss, both[:, :144], both[:, 144:]


def solution(mesh):
    placed = (P(("blk", "dp"), None), P(("blk", "dp"), None), P(), P())
    return jax.shard_map(
        body,
        mesh=mesh,
        in_specs=placed,
        out_specs=(P(("blk", "dp")), P("dp", "blk"), P("dp", "blk")),
        check_vma=False,
    )
```

time: 726 us -> 178 us (0.25)
  waiting for transfers between devices: 666 us -> 60.7 us
  matrix products: 26 us -> 64.6 us
  starting transfers between devices: 11.7 us -> 27.1 us
  between operations: 14.6 us -> 0.94 us
  other arithmetic: 1.72 us -> 11.1 us
    ppermute x5 -> x8, waiting for transfers between devices: 281 us -> 10.4 us  [the longest x4 10.4 us: blk_move(): return lax.ppermute(value, 'blk', pairs)]
    unnamed x4 -> x0, waiting for transfers between devices: 265 us -> none
    reduce_scatter x2 -> x0, waiting for transfers between devices: 120 us -> none  [the longest x1 120 us: body(): lax.psum_scatter(text_terms, 'blk', scatter_dimension=1, tiled=True)]
    all_to_all x0 -> x3, waiting for transfers between devices: none -> 50.2 us  [the longest x1 26.8 us: body(): both = lax.all_to_all(both, 'dp', 0, 0, axis_index_groups=groups).sum(0)]
    dot_general x13 -> x20, matrix products: 26 us -> 64.6 us  [the longest x6 23.5 us: pair_weights(): lax.dot_general(mine, theirs, (((1,), (1,)), ((), ())), preferred_element...]
    all_to_all x0 -> x3, starting transfers between devices: none -> 22.9 us  [the longest x2 12.3 us: head_terms(): return lax.all_to_all(terms, 'blk', 0, 0)]
    ppermute x5 -> x8, starting transfers between devices: 11.6 us -> 4.17 us  [the longest x4 4.07 us: blk_move(): return lax.ppermute(value, 'blk', pairs)]
  transfers between devices with their start and end apart: 8 -> 11, of which waited for: 7 -> 5; matrix products, arithmetic and copies ran while one was open for 2% -> 38% of each run, Pallas kernels for 0% -> 0%
where the time goes in v1:
time: 178 us; the launch traced here: 177 us
  matrix products  64.6 us (36%)
  waiting for transfers between devices  60.7 us (34%)
  starting transfers between devices  27.1 us (15%)
  local copies, waits for them, and re-layouts  12.2 us (7%)
  other arithmetic  11.1 us (6%)
    all_to_all x1, waiting for transfers between devices, body(): both = lax.all_to_all(both, 'dp', 0, 0, axis_index_groups=groups).sum(0)  26.8 us
    dot_general x6, matrix products, pair_weights(): lax.dot_general(mine, theirs, (((1,), (1,)), ((), ())), preferred_element...  23.5 us
    all_to_all x2, waiting for transfers between devices, head_terms(): return lax.all_to_all(terms, 'blk', 0, 0)  23.4 us
    dot_general x6, matrix products, side(): grad = grad + jnp.dot(weights, theirs, preferred_element_type=F32)  15.6 us
    dot_general x4, matrix products, row_dot(): lax.dot_general(left, right, (((0,), (0,)), ((), ())), preferred_element_...  14.9 us
    all_to_all x2, starting transfers between devices, head_terms(): return lax.all_to_all(terms, 'blk', 0, 0)  12.3 us
    all_to_all x1, starting transfers between devices, body(): both = lax.all_to_all(both, 'dp', 0, 0, axis_index_groups=groups).sum(0)  10.6 us
    ppermute x4, waiting for transfers between devices, blk_move(): return lax.ppermute(value, 'blk', pairs)  10.4 us
  transfers between devices with their start and end apart: 11, of which 5 were waited for; matrix products, arithmetic and copies ran while one was open for 38% of the time, Pallas kernels for 0%

profile of v1, /device:TPU:10, one launch (start us, length us, event | category | flops | bytes accessed | tf_op | source)
XLA Modules:
  0.0 176.6 jit_solution(10798808612064444069)
XLA Ops:
  2.4 3.4 %multiply_reduce_fusion.3 = (f32[512]{0:T(512)S(1)}, f32[512,1152]{1,0:T(8,128)S(1)}) fusion(bf16[512,1152]{1,0:T(8,128)(2,1)} %param.4, bf16[1152,1152]{1,0:T(8,128)(2,1)S(1)} %copy-done), kind=kOutput, calls=%fused_computation.28 | convolution fusion | flops 1360133632 | bytes 6195200 | tf_op jit(solution)/shard_map/dot_general | solution.py:14
  7.7 2.6 %fusion.76 = (bf16[512,1152]{1,0:T(8,128)(2,1)S(1)}, f32[512,1152]{1,0:T(8,128)S(1)}, bf16[512,1152]{1,0:T(8,128)(2,1)}, f32[512,1152]{1,0:T(8,128)}) fusion(f32[512,1152]{1,0:T(8,128)S(1)} %get-tuple-element.20, f32[512]{0:T(512)S(1)} %get-tuple-element.15, f32[512,1152]{1,0:T(8,128)S(1)} %get-tuple-element.18, f32[512]{0:T(512)S(1)} %get-tuple-element.16, ...), kind=kLoop, calls=%fused_computation.131 | loop fusion | flops 3538944 | bytes 11800577 | tf_op jit(solution)/shard_map/convert_element_type | solution.py:79
  14.2 3.3 %convolution_convert_fusion.2 = bf16[512,576]{0,1:T(8,128)(2,1)} fusion(bf16[512,1152]{1,0:T(8,128)(2,1)} %param.5, bf16[512,1152]{1,0:T(8,128)(2,1)} %param.4, pred[]{:T(512)S(6)} %eq.33, s32[]{:T(128)S(6)} %mul.104, s32[576]{0:T(1024)S(1)} %get-tuple-element.38, s32[576]{0:T(1024)} %get-tuple-element.39, s32[576]{0:T(1024)S(1)} %get-tuple-element.37, ...), kind=kOutput, calls=%fused_computation.50 | convolution fusion | flops 684343296 | bytes 2959493 | tf_op jit(solution)/shard_map/dot_general | solution.py:65
  17.5 4.2 %fusion.31 = (f32[512]{0:T(512)}, f32[512,512]{0,1:T(8,128)}) fusion(bf16[512,1152]{1,0:T(8,128)(2,1)} %get-tuple-element.7, bf16[512,1152]{1,0:T(8,128)(2,1)S(1)} %get-tuple-element.3), kind=kOutput, calls=%fused_computation.74 | convolution fusion | flops 607387136 | bytes 3409920 | tf_op jit(solution)/shard_map/dot_general | solution.py:31
  21.8 4.2 %fusion.28 = (f32[512]{0:T(512)}, f32[512,512]{0,1:T(8,128)}) fusion(bf16[512,1152]{1,0:T(8,128)(2,1)S(1)} %get-tuple-element.3, bf16[512,1152]{1,0:T(8,128)(2,1)} %get-tuple-element.7), kind=kOutput, calls=%fused_computation.71 | convolution fusion | flops 607387136 | bytes 3409920 | tf_op jit(solution)/shard_map/dot_general | solution.py:31
  28.2 3.6 %fusion.35 = f32[512,1152]{1,0:T(8,128)} fusion(bf16[512,1152]{1,0:T(8,128)(2,1)} %get-tuple-element.7, f32[512,512]{0,1:T(8,128)S(1)} %copy-done.22), kind=kOutput, calls=%fused_computation.85 | convolution fusion | flops 606601216 | bytes 4587520 | tf_op jit(solution)/shard_map/dot_general | solution.py:48
  31.9 8.0 %collective-permute-done = bf16[512,1152]{1,0:T(8,128)(2,1)} collective-permute-done((bf16[512,1152]{1,0:T(8,128)(2,1)S(1)}, bf16[512,1152]{1,0:T(8,128)(2,1)}, u32[]{:S(2)}, u32[]{:S(2)}) %collective-permute-start) | collective-permute-done | bytes 1179680 | tf_op jit(solution)/shard_map/ppermute | solution.py:22
  41.2 3.6 %fusion.33 = (f32[512]{0:T(512)}, f32[512,512]{0,1:T(8,128)S(1)}) fusion(bf16[512,1152]{1,0:T(8,128)(2,1)} %get-tuple-element.7, bf16[512,1152]{1,0:T(8,128)(2,1)} %collective-permute-done), kind=kOutput, calls=%fused_computation.76 | convolution fusion | flops 606862848 | bytes 3409920 | tf_op jit(solution)/shard_map/dot_general | solution.py:31
  44.8 3.6 %fusion.32 = (f32[512]{0:T(512)}, f32[512,512]{0,1:T(8,128)S(1)}) fusion(bf16[512,1152]{1,0:T(8,128)(2,1)} %get-tuple-element.7, bf16[512,1152]{1,0:T(8,128)(2,1)} %collective-permute-done.3), kind=kOutput, calls=%fused_computation.75 | convolution fusion | flops 606862848 | bytes 3409920 | tf_op jit(solution)/shard_map/dot_general | solution.py:31
  50.8 2.5 %multiply_reduce_fusion.1 = (f32[512]{0:T(512)S(1)}, f32[512,1152]{1,0:T(8,128)S(1)}) fusion(f32[512,1152]{1,0:T(8,128)S(1)} %copy-done.2, f32[512,1152]{1,0:T(8,128)S(1)} %convolution_add_fusion.5, bf16[512,1152]{1,0:T(8,128)(2,1)} %collective-permute-done, f32[512,512]{0,1:T(8,128)S(1)} %get-tuple-element.22), kind=kOutput, calls=%fused_computation.26 | convolution fusion | flops 607649280 | bytes 9308160 | tf_op jit(solution)/shard_map/dot_general | solution.py:48
  54.6 4.2 %fusion.30 = (f32[512]{0:T(512)}, f32[512,512]{0,1:T(8,128)}) fusion(bf16[512,1152]{1,0:T(8,128)(2,1)S(1)} %copy-done.6, bf16[512,1152]{1,0:T(8,128)(2,1)} %collective-permute-done.2), kind=kOutput, calls=%fused_computation.73 | convolution fusion | flops 606862848 | bytes 3409920 | tf_op jit(solution)/shard_map/dot_general | solution.py:31
  58.8 4.7 %fusion.16 = f32[1152,576]{0,1:T(8,128)} fusion(bf16[512,1152]{1,0:T(8,128)(2,1)S(1)} %divide_convert_fusion.1, bf16[512,1152]{1,0:T(8,128)(2,1)} %param.5, bf16[512,1152]{1,0:T(8,128)(2,1)} %param.4, pred[]{:T(512)S(6)} %eq.33, s32[576]{0:T(1024)S(1)} %get-tuple-element.38, s32[576]{0:T(1024)S(1)} %copy-done.7, s32[]{:T(128)S(6)} %mul.103, ...), kind=kOutput, calls=%fused_computation.59 | convolution fusion | flops 1363820544 | bytes 6203525 | tf_op jit(solution)/shard_map/dot_general | solution.py:57
  63.6 2.4 %collective-permute-done.1 = bf16[512,1152]{1,0:T(8,128)(2,1)} collective-permute-done((bf16[512,1152]{1,0:T(8,128)(2,1)}, bf16[512,1152]{1,0:T(8,128)(2,1)}, u32[]{:S(2)}, u32[]{:S(2)}) %collective-permute-start.1) | collective-permute-done | bytes 1179680 | tf_op jit(solution)/shard_map/ppermute | solution.py:22
  66.0 3.6 %fusion.29 = (f32[512]{0:T(512)}, f32[512,512]{0,1:T(8,128)S(1)}) fusion(bf16[512,1152]{1,0:T(8,128)(2,1)} %copy-done.5, bf16[512,1152]{1,0:T(8,128)(2,1)} %collective-permute-done.1), kind=kOutput, calls=%fused_computation.72 | convolution fusion | flops 606862848 | bytes 3409920 | tf_op jit(solution)/shard_map/dot_general | solution.py:31
  72.0 2.5 %multiply_reduce_fusion = (f32[512]{0:T(512)S(1)}, f32[512,1152]{1,0:T(8,128)S(1)}) fusion(f32[512,1152]{1,0:T(8,128)S(1)} %get-tuple-element.4, f32[512,1152]{1,0:T(8,128)S(1)} %convolution_add_fusion.3, bf16[512,1152]{1,0:T(8,128)(2,1)} %collective-permute-done.2, f32[512,512]{0,1:T(8,128)S(1)} %copy-done.20), kind=kOutput, calls=%fused_computation.24 | convolution fusion | flops 607649280 | bytes 9308160 | tf_op jit(solution)/shard_map/dot_general | solution.py:48
  80.7 6.7 %all-to-all-start = ((bf16[8,144,576]{2,1,0:T(8,128)(2,1)}), bf16[8,144,576]{2,1,0:T(8,128)(2,1)S(1)}, u32[]{:S(2)}, u32[]{:S(2)}) async-start(bf16[8,144,576]{2,1,0:T(8,128)(2,1)} %bitcast), calls=%async_computation | async-start | bytes 2949120 | tf_op jit(solution)/shard_map/all_to_all | solution.py:98
  89.5 4.7 %fusion.17 = f32[1152,576]{0,1:T(8,128)} fusion(bf16[512,1152]{1,0:T(8,128)(2,1)} %divide_convert_fusion, bf16[512,1152]{1,0:T(8,128)(2,1)} %param.4, bf16[512,1152]{1,0:T(8,128)(2,1)S(1)} %copy-done.19, pred[]{:T(512)S(6)} %eq.33, s32[576]{0:T(1024)S(1)} %get-tuple-element.38, s32[576]{0:T(1024)S(1)} %copy-done.7, s32[]{:T(128)S(6)} %mul.103, ...), kind=kOutput, calls=%fused_computation.60 | convolution fusion | flops 1363820544 | bytes 6203525 | tf_op jit(solution)/shard_map/dot_general | solution.py:57
  94.2 3.0 %fusion.3 = bf16[1152,576]{0,1:T(8,128)(2,1)S(1)} fusion(f32[1152,576]{0,1:T(8,128)} %fusion.17, bf16[512,576]{0,1:T(8,128)(2,1)S(1)} %collective-permute-done.7, bf16[512,1152]{1,0:T(8,128)(2,1)} %collective-permute-done.6), kind=kOutput, calls=%fused_computation.17 | convolution fusion | flops 680804352 | bytes 5750784 | tf_op jit(solution)/shard_map/dot_general | solution.py:57
  98.9 7.0 %all-to-all-done = bf16[8,144,576]{2,1,0:T(8,128)(2,1)S(1)} async-done(((bf16[8,144,576]{2,1,0:T(8,128)(2,1)}), bf16[8,144,576]{2,1,0:T(8,128)(2,1)S(1)}, u32[]{:S(2)}, u32[]{:S(2)}) %all-to-all-start) | async-done | bytes 1327136 | tf_op jit(solution)/shard_map/all_to_all | solution.py:98
  105.9 5.6 %all-to-all-start.1 = ((bf16[8,144,576]{2,1,0:T(8,128)(2,1)}), bf16[8,144,576]{2,1,0:T(8,128)(2,1)S(1)}, u32[]{:S(2)}, u32[]{:S(2)}) async-start(bf16[8,144,576]{2,1,0:T(8,128)(2,1)} %bitcast.2), calls=%async_computation.1 | async-start | bytes 2949120 | tf_op jit(solution)/shard_map/all_to_all | solution.py:98
  112.6 16.5 %all-to-all-done.1 = bf16[8,144,576]{2,1,0:T(8,128)(2,1)S(1)} async-done(((bf16[8,144,576]{2,1,0:T(8,128)(2,1)}), bf16[8,144,576]{2,1,0:T(8,128)(2,1)S(1)}, u32[]{:S(2)}, u32[]{:S(2)}) %all-to-all-start.1) | async-done | bytes 1327136 | tf_op jit(solution)/shard_map/all_to_all | solution.py:98
  133.1 3.4 %reshape.55 = f32[16,36,288]{2,1,0:T(8,128)} reshape(f32[16,36,2,144]{3,2,1,0:T(2,128)} %maximum_bitcast_fusion) | data formatting | bytes 1327104 | tf_op jit(solution)/shard_map/reshape | solution.py:108
  136.5 10.6 %all-to-all-start.2 = ((f32[16,36,288]{2,1,0:T(8,128)}), f32[16,36,288]{2,1,0:T(8,128)}, u32[]{:S(2)}, u32[]{:S(2)}) async-start(f32[16,36,288]{2,1,0:T(8,128)} %reshape.55), calls=%async_computation.2 | async-start | bytes 1966080 | tf_op jit(solution)/shard_map/all_to_all | solution.py:110
  147.8 26.8 %all-to-all-done.2 = f32[16,36,288]{2,1,0:T(8,128)} async-done(((f32[16,36,288]{2,1,0:T(8,128)}), f32[16,36,288]{2,1,0:T(8,128)}, u32[]{:S(2)}, u32[]{:S(2)}) %all-to-all-start.2) | async-done | bytes 663584 | tf_op jit(solution)/shard_map/all_to_all | solution.py:110
  (83 shorter events, 34.7 us)
Async XLA Ops:
  10.4 15.6 %copy-start.5 = (bf16[512,1152]{1,0:T(8,128)(2,1)}, bf16[512,1152]{1,0:T(8,128)(2,1)S(1)}, u32[]{:S(2)}) copy-start(bf16[512,1152]{1,0:T(8,128)(2,1)S(1)} %get-tuple-element.3) | copy-start | bytes 3538948
  10.4 34.5 %collective-permute-start.3 = (bf16[512,1152]{1,0:T(8,128)(2,1)}, bf16[512,1152]{1,0:T(8,128)(2,1)}, u32[]{:S(2)}, u32[]{:S(2)}) collective-permute-start(bf16[512,1152]{1,0:T(8,128)(2,1)} %get-tuple-element.7), channel_id=1, source_target_pairs={{0,32},{32,0},{64,96},{96,64},{128,160},{160,128},{192,224},{224,1... | collective-permute-start | bytes 3538952 | tf_op jit(solution)/shard_map/ppermute | solution.py:22
  10.9 42.9 %collective-permute-start.2 = (bf16[512,1152]{1,0:T(8,128)(2,1)}, bf16[512,1152]{1,0:T(8,128)(2,1)}, u32[]{:S(2)}, u32[]{:S(2)}) collective-permute-start(bf16[512,1152]{1,0:T(8,128)(2,1)} %get-tuple-element.7), channel_id=1, source_target_pairs={{0,64},{32,224},{64,128},{96,32},{128,192},{160,96},{192,0},{224,1... | collective-permute-start | bytes 3538952 | tf_op jit(solution)/shard_map/ppermute | solution.py:22
  13.1 26.8 %collective-permute-start = (bf16[512,1152]{1,0:T(8,128)(2,1)S(1)}, bf16[512,1152]{1,0:T(8,128)(2,1)}, u32[]{:S(2)}, u32[]{:S(2)}) collective-permute-start(bf16[512,1152]{1,0:T(8,128)(2,1)S(1)} %get-tuple-element.3), channel_id=1, source_target_pairs={{0,192},{32,96},{64,0},{96,160},{128,64},{160,224},{192,128},{224,... | collective-permute-start | bytes 3538952 | tf_op jit(solution)/shard_map/ppermute | solution.py:22
  17.5 58.4 %collective-permute-start.5 = (bf16[512,576]{0,1:T(8,128)(2,1)}, bf16[512,576]{0,1:T(8,128)(2,1)}, u32[]{:S(2)}, u32[]{:S(2)}) collective-permute-start(bf16[512,576]{0,1:T(8,128)(2,1)} %convolution_convert_fusion.2), channel_id=1, source_target_pairs={{0,1},{1,0},{2,3},{3,2},{4,5},{5,4},{6,7},{7,6},{8,9},{9,8},{10,11... | collective-permute-start | bytes 1769480 | tf_op jit(solution)/shard_map/ppermute | solution.py:27
  39.9 26.1 %collective-permute-start.1 = (bf16[512,1152]{1,0:T(8,128)(2,1)}, bf16[512,1152]{1,0:T(8,128)(2,1)}, u32[]{:S(2)}, u32[]{:S(2)}) collective-permute-start(bf16[512,1152]{1,0:T(8,128)(2,1)} %collective-permute-done), channel_id=1, source_target_pairs={{0,32},{32,0},{64,96},{96,64},{128,160},{160,128},{192,224},{224,1... | collective-permute-start | bytes 3538952 | tf_op jit(solution)/shard_map/ppermute | solution.py:22
  53.7 22.2 %collective-permute-start.4 = (bf16[512,1152]{1,0:T(8,128)(2,1)S(1)}, bf16[512,1152]{1,0:T(8,128)(2,1)}, u32[]{:S(2)}, u32[]{:S(2)}) collective-permute-start(bf16[512,1152]{1,0:T(8,128)(2,1)S(1)} %divide_convert_fusion.1), channel_id=1, source_target_pairs={{0,1},{1,0},{2,3},{3,2},{4,5},{5,4},{6,7},{7,6},{8,9},{9,8},{10,11... | collective-permute-start | bytes 3538952 | tf_op jit(solution)/shard_map/ppermute | solution.py:27
  75.9 18.3 %collective-permute-start.6 = (bf16[512,1152]{1,0:T(8,128)(2,1)}, bf16[512,1152]{1,0:T(8,128)(2,1)}, u32[]{:S(2)}, u32[]{:S(2)}) collective-permute-start(bf16[512,1152]{1,0:T(8,128)(2,1)} %divide_convert_fusion), channel_id=1, source_target_pairs={{0,1},{1,0},{2,3},{3,2},{4,5},{5,4},{6,7},{7,6},{8,9},{9,8},{10,11... | collective-permute-start | bytes 3538952 | tf_op jit(solution)/shard_map/ppermute | solution.py:27
  80.7 6.7 %copy-start.8 = (s32[576]{0:T(1024)S(1)}, s32[576]{0:T(1024)}, u32[]{:S(2)}) copy-start(s32[576]{0:T(1024)} %get-tuple-element.40) | copy-start | bytes 6916
  80.7 6.7 %copy-start.15 = (pred[576]{0:T(1024)(128)(4,1)S(1)}, pred[576]{0:T(1024)(128)(4,1)}, u32[]{:S(2)}) copy-start(pred[576]{0:T(1024)(128)(4,1)} %get-tuple-element.41) | copy-start | bytes 1732
  80.7 6.7 %copy-start.16 = (pred[576]{0:T(1024)(128)(4,1)S(1)}, pred[576]{0:T(1024)(128)(4,1)}, u32[]{:S(2)}) copy-start(pred[576]{0:T(1024)(128)(4,1)} %get-tuple-element.42) | copy-start | bytes 1732
  80.7 6.7 %copy-start.19 = (bf16[512,1152]{1,0:T(8,128)(2,1)S(1)}, bf16[512,1152]{1,0:T(8,128)(2,1)}, u32[]{:S(2)}) copy-start(bf16[512,1152]{1,0:T(8,128)(2,1)} %param.5) | copy-start | bytes 3538948
  80.7 25.2 %all-to-all-start = ((bf16[8,144,576]{2,1,0:T(8,128)(2,1)}), bf16[8,144,576]{2,1,0:T(8,128)(2,1)S(1)}, u32[]{:S(2)}, u32[]{:S(2)}) async-start(bf16[8,144,576]{2,1,0:T(8,128)(2,1)} %bitcast), calls=%async_computation | async-start | bytes 2949120 | tf_op jit(solution)/shard_map/all_to_all | solution.py:98
  89.5 4.7 %collective-permute-start.7 = (bf16[512,576]{0,1:T(8,128)(2,1)}, bf16[512,576]{0,1:T(8,128)(2,1)S(1)}, u32[]{:S(2)}, u32[]{:S(2)}) collective-permute-start(bf16[512,576]{0,1:T(8,128)(2,1)} %convolution_convert_fusion), channel_id=1, source_target_pairs={{0,1},{1,0},{2,3},{3,2},{4,5},{5,4},{6,7},{7,6},{8,9},{9,8},{10,11... | collective-permute-start | bytes 1769480 | tf_op jit(solution)/shard_map/ppermute | solution.py:27
  105.9 23.2 %all-to-all-start.1 = ((bf16[8,144,576]{2,1,0:T(8,128)(2,1)}), bf16[8,144,576]{2,1,0:T(8,128)(2,1)S(1)}, u32[]{:S(2)}, u32[]{:S(2)}) async-start(bf16[8,144,576]{2,1,0:T(8,128)(2,1)} %bitcast.2), calls=%async_computation.1 | async-start | bytes 2949120 | tf_op jit(solution)/shard_map/all_to_all | solution.py:98
  112.6 16.7 %copy-start.3 = (f32[2,144,576]{2,1,0:T(8,128)S(1)}, f32[2,144,576]{2,1,0:T(8,128)}, u32[]{:S(2)}) copy-start(f32[2,144,576]{2,1,0:T(8,128)} %convert_reduce_fusion.1) | copy-start | bytes 1990660
  133.1 43.5 %copy-start.1 = (bf16[1152,1152]{1,0:T(8,128)(2,1)S(1)}, bf16[1152,1152]{1,0:T(8,128)(2,1)}, u32[]{:S(2)}) copy-start(bf16[1152,1152]{1,0:T(8,128)(2,1)} %param.6) | copy-start | bytes 7962628
  136.5 10.7 %copy-start.9 = (f32[512]{0:T(512)S(1)}, f32[512]{0:T(512)}, u32[]{:S(2)}) copy-start(f32[512]{0:T(512)} %get-tuple-element.23) | copy-start | bytes 6148
  136.5 10.7 %copy-start.10 = (f32[512]{0:T(512)S(1)}, f32[512]{0:T(512)}, u32[]{:S(2)}) copy-start(f32[512]{0:T(512)} %get-tuple-element.29) | copy-start | bytes 6148
  136.5 10.7 %copy-start.11 = (f32[512]{0:T(512)S(1)}, f32[512]{0:T(512)}, u32[]{:S(2)}) copy-start(f32[512]{0:T(512)} %get-tuple-element.21) | copy-start | bytes 6148
  136.5 10.7 %copy-start.12 = (f32[512]{0:T(512)S(1)}, f32[512]{0:T(512)}, u32[]{:S(2)}) copy-start(f32[512]{0:T(512)} %get-tuple-element.25) | copy-start | bytes 6148
  136.5 10.7 %copy-start.13 = (f32[512]{0:T(512)S(1)}, f32[512]{0:T(512)}, u32[]{:S(2)}) copy-start(f32[512]{0:T(512)} %get-tuple-element.27) | copy-start | bytes 6148
  136.5 10.7 %copy-start.14 = (f32[512]{0:T(512)S(1)}, f32[512]{0:T(512)}, u32[]{:S(2)}) copy-start(f32[512]{0:T(512)} %get-tuple-element.31) | copy-start | bytes 6148
  136.5 38.1 %all-to-all-start.2 = ((f32[16,36,288]{2,1,0:T(8,128)}), f32[16,36,288]{2,1,0:T(8,128)}, u32[]{:S(2)}, u32[]{:S(2)}) async-start(f32[16,36,288]{2,1,0:T(8,128)} %reshape.55), calls=%async_computation.2 | async-start | bytes 1966080 | tf_op jit(solution)/shard_map/all_to_all | solution.py:110
  (10 other events, 30.1 us)

commit v2 on v0

v2 whole, which is shorter than its diff:
```python
import functools
import math

import jax
import jax.numpy as jnp
from jax import lax
from jax.experimental import pallas as pl
from jax.experimental.pallas import tpu as pltpu
from jax.sharding import Mesh
from jax.sharding import PartitionSpec as P

TEMP = 30.0
BIAS = -6.0
EPS = 1e-06
LOG2E = math.log2(math.e)
F32 = jnp.float32
BF16 = jnp.bfloat16
D = 1152
ROWS = 512
AXES = ("y", "xlo", "xhi", "z", "core")
SIZES = (4, 2, 2, 8, 2)
MIB = 1024 * 1024
EMBED_VMEM = 52
NT = (((1,), (1,)), ((), ()))

VMEM = functools.partial(pl.BlockSpec, memory_space=pltpu.VMEM)
SMEM = functools.partial(pl.BlockSpec, memory_space=pltpu.SMEM)
HBM = functools.partial(pl.BlockSpec, memory_space=pltpu.HBM)


def shape(dims, dtype):
    return jax.ShapeDtypeStruct(dims, dtype)


def call(kernel, name, ins, outs, out_specs=None, scratch=(), vmem=20):
    if out_specs is None:
        out_specs = jax.tree.map(lambda _: VMEM(), outs)
    return pl.pallas_call(
        kernel,
        name=name,
        in_specs=ins,
        out_shape=outs,
        out_specs=out_specs,
        scratch_shapes=list(scratch),
        compiler_params=pltpu.CompilerParams(vmem_limit_bytes=vmem * MIB),
        cost_estimate=pl.CostEstimate(flops=1000, bytes_accessed=1000, transcendentals=0),
    )


def embed_kernel(odd, image_feats, text_feats, image_head, text_head, *refs):
    outs, (feats, head, held, in_sems, out_sems) = refs[:6], refs[6:]
    cut = 3
    width = D // cut

    def loads(side, src_feats, src_head):
        yield pltpu.make_async_copy(src_feats, feats.at[side], in_sems.at[side, cut])
        for j in range(cut):
            cols = pl.ds(j * width, width)
            yield pltpu.make_async_copy(src_head.at[:, cols], head.at[side, :, cols], in_sems.at[side, j])

    for value in range(2):

        @pl.when(odd[0] == value)
        def _(value=value):
            order = ((text_feats, text_head), (image_feats, image_head))
            for side in range(2):
                for copy in loads(side, *order[side ^ value]):
                    copy.start()

    saves = []
    for side in range(2):
        emb, proj_out, norm = outs[3 * side : 3 * side + 3]
        waits = list(loads(side, image_feats, image_head))
        waits[0].wait()
        total = jnp.zeros((ROWS, 1), F32)
        for j in range(cut):
            cols = pl.ds(j * width, width)
            waits[j + 1].wait()
            proj = jnp.dot(feats[side], head[side, :, cols], preferred_element_type=F32)
            held[side, :, cols] = proj
            saves.append(pltpu.make_async_copy(held.at[side, :, cols], proj_out.at[:, cols], out_sems.at[side, j]))
            saves[-1].start()
            total += jnp.sum(proj * proj, axis=1, keepdims=True)
        length = jnp.sqrt(total + EPS)
        norm[...] = length
        emb[...] = (held[side] * (1.0 / length)).astype(BF16)
    for copy in saves:
        copy.wait()


def embed(odd, image_feats, text_feats, image_head, text_head):
    one = [shape((ROWS, D), BF16), shape((ROWS, D), F32), shape((ROWS, 1), F32)]
    return call(
        embed_kernel,
        "embed",
        [SMEM(), HBM(), HBM(), HBM(), HBM()],
        one + one,
        out_specs=[VMEM(), HBM(), VMEM()] * 2,
        scratch=[
            pltpu.VMEM((2, ROWS, D), BF16),
            pltpu.VMEM((2, D, D), BF16),
            pltpu.VMEM((2, ROWS, D), F32),
            pltpu.SemaphoreType.DMA((2, 4)),
            pltpu.SemaphoreType.DMA((2, 3)),
        ],
        vmem=EMBED_VMEM,
    )(odd, image_feats, text_feats, image_head, text_head)


def add_pair(mine, theirs, rows, diagonal):
    dots = lax.dot_general(mine[rows, :], theirs[...], NT, preferred_element_type=F32)
    grow = dots * (-TEMP * LOG2E) + (-BIAS * LOG2E)
    if diagonal:
        row = lax.broadcasted_iota(jnp.int32, dots.shape, 0) + rows.start
        eye = row == lax.broadcasted_iota(jnp.int32, dots.shape, 1)
        grow = jnp.where(eye, -grow, grow)
    weights = 1.0 / (float(ROWS) + jnp.exp2(grow + math.log2(ROWS)))
    if diagonal:
        weights = jnp.where(eye, -weights, weights)
    return jnp.dot(weights.astype(BF16), theirs[...], preferred_element_type=F32)


def side_kernel(count, diagonal, last, *refs):
    mine, partners, rest = refs[0], refs[1 : 1 + count], refs[1 + count :]
    if last:
        before, proj, norm, out = rest
    else:
        (out,) = rest
    block = 256
    for i in range(ROWS // block):
        rows = pl.ds(i * block, block)
        grad = before[rows, :] if last else None
        for step, theirs in enumerate(partners):
            part = add_pair(mine, theirs, rows, diagonal and step == 0)
            grad = part if grad is None else grad + part
        if last:
            grad = TEMP * grad
            inverse = 1.0 / norm[rows, :]
            own = proj[rows, :] * inverse
            along = jnp.sum(own * grad, axis=1, keepdims=True)
            value = (grad - own * along) * inverse
            out[:, rows] = value.T.astype(BF16)
        else:
            out[rows, :] = grad


def side(mine, partners, diagonal, before=None, proj=None, norm=None):
    last = before is not None
    args = [mine, *partners] + ([before, proj, norm] if last else [])
    return call(
        functools.partial(side_kernel, len(partners), diagonal, last),
        "side_last" if last else "side_first",
        [VMEM()] * len(args),
        shape((D, ROWS), BF16) if last else shape((ROWS, D), F32),
    )(*args)


def loss_kernel(use_a, a_emb, b_emb, a_cross, b_cross, a_from, b_from, out):
    def total(mine, partners):
        result = jnp.zeros((1, ROWS), F32)
        for step, theirs in enumerate(partners):
            for i in range(2):
                rows = pl.ds(i * 256, 256)
                z = TEMP * lax.dot_general(theirs[rows, :], mine[...], NT, preferred_element_type=F32) + BIAS
                if step == 0:
                    row = lax.broadcasted_iota(jnp.int32, z.shape, 0) + i * 256
                    z = jnp.where(row == lax.broadcasted_iota(jnp.int32, z.shape, 1), -z, z)
                soft = jnp.maximum(z, 0.0) + jnp.log1p(jnp.exp(-jnp.abs(z)))
                result += jnp.sum(soft, axis=0, keepdims=True)
        out[...] = result

    @pl.when(use_a[0] == 1)
    def _():
        total(a_emb, (b_emb, a_cross, b_from))

    @pl.when(use_a[0] != 1)
    def _():
        total(b_emb, (a_emb, b_cross, a_from))


def head_own_kernel(grad, feats, out):
    out[...] = jnp.dot(grad[...], feats[...], preferred_element_type=F32)


def head_pack_kernel(grad, feats, before, out):
    for y in range(4):
        rows = pl.ds(y * 288, 288)
        terms = before[rows, :] + jnp.dot(grad[rows, :], feats[...], preferred_element_type=F32)
        for xhi in range(2):
            base = xhi * 384
            chunk = 2 * y + xhi
            out[chunk, 0:288, :] = terms[:, base : base + 128].astype(BF16)
            out[chunk, 288:576, :] = terms[:, base + 128 : base + 256].astype(BF16)
            few = terms[:, base + 256 : base + 384]
            few = few[0:96] + pltpu.roll(few[96:192], 32, 1) + pltpu.roll(few[192:288], 64, 1)
            out[chunk, 576:672, :] = few.astype(BF16)


def repack(total, store):
    lane = lax.broadcasted_iota(jnp.int32, (48, 128), 1)
    for z in range(8):
        for xlo in range(2):
            value = jnp.zeros((48, 128), F32)
            for g in range(3):
                m = xlo * 144 + g * 48
                wide = total[(z // 4) * 288 + m : (z // 4) * 288 + m + 48, :]
                move = (32 * g - 32 * (z % 4)) % 128
                wide = pltpu.roll(wide, move, 1) if move else wide
                value = jnp.where((lane >= 32 * g) & (lane < 32 * g + 32), wide, value)
                group, row = m // 96, m % 96
                few = total[576 + row : 576 + row + 48, :]
                move = (96 + 4 * g - 32 * group - 4 * z) % 128
                few = pltpu.roll(few, move, 1) if move else few
                first = 96 + 4 * g
                value = jnp.where((lane >= first) & (lane < first + 4), few, value)
            store(z, xlo, value)


def add_y_kernel(xhi, got, keep, give):
    def total(which):
        value = got[0, which].astype(F32)
        for s in range(1, 4):
            value = value + got[s, which].astype(F32)
        return value

    keep[...] = total(xhi[0])
    give[...] = total(1 - xhi[0]).astype(BF16)


def add_pack_kernel(a_keep, a_take, b_got, out):
    a_total = a_keep[...] + a_take[...].astype(F32)
    b_total = b_got[0].astype(F32)
    for s in range(1, 8):
        b_total = b_total + b_got[s].astype(F32)
    for side, total in enumerate((a_total, b_total)):

        def store(z, xlo, value, side=side):
            out[z, xlo, side] = value.astype(BF16)

        repack(total, store)


def finish_kernel(got, image, text):
    for out, parity in ((text, 0), (image, 1)):
        value = jnp.zeros((48, 128), F32)
        for z in range(8):
            value = value + got[z, parity, 0].astype(F32) + got[z, 1 - parity, 1].astype(F32)
        turned = value.T
        parts = []
        for g in range(3):
            parts.append(jnp.concatenate([turned[32 * g : 32 * g + 32], turned[96 + 4 * g : 100 + 4 * g]], axis=0))
        out[...] = jnp.concatenate(parts, axis=1)


def position(coords):
    index = 0
    for coord, size in zip(coords, SIZES):
        index = index * size + coord % size
    return index


def move(value, target):
    pairs = []
    for source in range(math.prod(SIZES)):
        rest, coords = source, []
        for size in reversed(SIZES):
            coords.insert(0, rest % size)
            rest //= size
        pairs.append((source, position(target(*coords))))
    return lax.ppermute(value, AXES, pairs)


def swap_x(value):
    return move(value, lambda y, xl, xh, z, c: (y, 1 - xl, xh, z, c))


def swap_core(value):
    return move(value, lambda y, xl, xh, z, c: (y, xl, xh, z, 1 - c))


def shift_y(value, even, odd):
    return move(value, lambda y, xl, xh, z, c: (y + (odd if xl else even), xl, xh, z, c))


def after(values, *earlier):
    return lax.optimization_barrier((*values, *earlier))[: len(values)]


def core_columns(core):
    row = lax.broadcasted_iota(jnp.int32, (D, 768), 0)
    col = lax.broadcasted_iota(jnp.int32, (D, 768), 1)
    xhi, lane = col // 384, col % 384
    few = lane >= 256
    z = jnp.where(few, (lane - 256) // 4, lane // 32)
    r = jnp.where(few, 32 + (lane - 256) % 4, lane % 32)
    source = jnp.where(lane < 288, xhi * 576 + z * 72 + core * 36 + r, -1)
    return (row == source).astype(BF16)


def body(image_feats, text_feats, image_head, text_head):
    odd = lax.axis_index("xlo")
    core = lax.axis_index("core")
    flag = odd.astype(jnp.int32).reshape(1)

    a_emb, a_proj, a_norm, b_emb, b_proj, b_norm = embed(flag, image_feats, text_feats, image_head, text_head)
    a_cross = swap_x(a_emb)
    b_from = shift_y(b_emb, -1, 1)
    a_from = shift_y(a_emb, 1, -1)

    def together(steps, *args):
        def nothing(*_):
            return jax.tree.map(lambda x: jnp.zeros(x.shape, x.dtype), jax.eval_shape(steps, *args))

        return lax.cond(flag[0] < 2, steps, nothing, *args)

    def prepare(image_feats, text_feats, a_emb, b_emb):
        own_columns, oth_columns = core_columns(core), core_columns(1 - core)
        a_feats = jnp.where(odd == 1, image_feats, text_feats)
        b_feats = jnp.where(odd == 1, text_feats, image_feats)

        def columns(feats):
            own = jnp.dot(feats, own_columns, preferred_element_type=F32).astype(BF16)
            oth = jnp.dot(feats, oth_columns, preferred_element_type=F32).astype(BF16)
            return own, swap_core(oth)

        return (*columns(a_feats), *columns(b_feats), side(a_emb, (b_emb,), True))

    a_own, a_oth, b_own, b_oth, a_first = together(prepare, image_feats, text_feats, a_emb, b_emb)
    b_from, a_from = after((b_from, a_from), a_own, b_own, a_oth, b_oth, a_first)
    b_cross = swap_x(b_from)

    def head_terms(mine, own, oth):
        theirs = swap_core(mine)
        before = call(head_own_kernel, "head_own", [VMEM()] * 2, shape((D, 768), F32))(mine, own)
        return call(head_pack_kernel, "head_pack", [VMEM()] * 3, shape((8, 672, 128), BF16))(theirs, oth, before)

    def finished(mine, partners, before, proj, norm, own, oth):
        return head_terms(side(mine, partners, False, before, proj, norm), own, oth)

    a_terms = together(finished, a_emb, (a_cross, b_from), a_first, a_proj, a_norm, a_own, a_oth)
    a_got = lax.all_to_all(a_terms.reshape(4, 2, 672, 128), "y", 0, 0)

    (a_from,) = after((a_from,), a_terms)
    b_first = side(b_emb, (a_emb, a_from), True)
    a_keep, a_give = call(
        add_y_kernel, "add_y", [SMEM(), VMEM()], [shape((672, 128), F32), shape((672, 128), BF16)]
    )(lax.axis_index("xhi").astype(jnp.int32).reshape(1), a_got)
    a_take = move(a_give, lambda y, xl, xh, z, c: (y, xl, 1 - xh, z, c))

    (b_cross,) = after((b_cross,), b_first)
    b_terms = together(finished, b_emb, (b_cross,), b_first, b_proj, b_norm, b_own, b_oth)
    b_got = lax.all_to_all(b_terms, ("y", "xhi"), 0, 0)

    (loss_emb,) = after((a_emb,), b_terms)
    row_loss = call(loss_kernel, "loss", [SMEM()] + [VMEM()] * 6, shape((1, ROWS), F32))(
        flag, loss_emb, b_emb, a_cross, b_cross, a_from, b_from
    )
    (b_got,) = after((b_got,), row_loss)
    part = call(add_pack_kernel, "add_pack", [VMEM()] * 3, shape((8, 2, 2, 48, 128), BF16))(a_keep, a_take, b_got)
    got = lax.all_to_all(part.reshape(16, 2, 48, 128), ("z", "xlo"), 0, 0).reshape(8, 2, 2, 48, 128)
    image_grad, text_grad = call(
        finish_kernel, "finish", [VMEM()], [shape((36, 144), F32), shape((36, 144), F32)]
    )(got)
    return row_loss.reshape(ROWS), image_grad, text_grad


def solution(mesh):
    fine = Mesh(mesh.devices.reshape(SIZES), AXES)
    blk, dp = ("y", "xlo"), ("xhi", "z", "core")
    placed = (P(AXES, None), P(AXES, None), P(), P())
    return jax.shard_map(
        body,
        mesh=fine,
        in_specs=placed,
        out_specs=(P(AXES), P(dp, blk), P(dp, blk)),
        check_vma=False,
    )
```

time: 726 us -> 133 us (0.18)
  waiting for transfers between devices: 666 us -> 21.8 us
  Pallas kernels: 0 us -> 51.8 us
  blocking collectives: 0 us -> 22.1 us
  between operations: 14.6 us -> 0.68 us
  matrix products: 26 us -> 12.4 us
  starting transfers between devices: 11.7 us -> 20.5 us
    ppermute x5 -> x9, waiting for transfers between devices: 281 us -> 13 us  [move(): return lax.ppermute(value, AXES, pairs)]
    unnamed x4 -> x0, waiting for transfers between devices: 265 us -> none
    reduce_scatter x2 -> x0, waiting for transfers between devices: 120 us -> none  [the longest x1 120 us: body(): lax.psum_scatter(text_terms, 'blk', scatter_dimension=1, tiled=True)]
    pallas_call x0 -> x13, Pallas kernels: none -> 51.8 us  [the longest x4 23.7 us: side(): call(functools.partial(side_kernel, len(partners), diagonal, last), 'side...]
    all_to_all x0 -> x1, blocking collectives: none -> 22.1 us  [body(): lax.all_to_all(part.reshape(16, 2, 48, 128), ('z', 'xlo'), 0, 0)]
    dot_general x13 -> x4, matrix products: 26 us -> 12.4 us  [the longest x2 6.6 us: columns(): oth = jnp.dot(feats, oth_columns, preferred_element_type=F32).astype(BF16)]
    all_to_all x0 -> x2, starting transfers between devices: none -> 13.1 us  [the longest x1 6.67 us: body(): b_got = lax.all_to_all(b_terms, ('y', 'xhi'), 0, 0)]
    all_to_all x0 -> x2, waiting for transfers between devices: none -> 8.83 us  [the longest x1 8.83 us: body(): b_got = lax.all_to_all(b_terms, ('y', 'xhi'), 0, 0)]
  transfers between devices with their start and end apart: 8 -> 11, of which waited for: 7 -> 6; matrix products, arithmetic and copies ran while one was open for 2% -> 9% of each run, Pallas kernels for 0% -> 31%
where the time goes in v2:
time: 133 us; the launch traced here: 131 us
  Pallas kernels  51.8 us (39%)
  blocking collectives  22.1 us (17%)
  waiting for transfers between devices  21.8 us (16%)
  starting transfers between devices  20.5 us (15%)
  matrix products  12.4 us (9%)
    pallas_call x4, Pallas kernels, side(): call(functools.partial(side_kernel, len(partners), diagonal, last), 'side...  23.7 us
    all_to_all x1, blocking collectives, body(): lax.all_to_all(part.reshape(16, 2, 48, 128), ('z', 'xlo'), 0, 0)  22.1 us
    ppermute x9, waiting for transfers between devices, move(): return lax.ppermute(value, AXES, pairs)  13 us
    pallas_call x1, Pallas kernels, embed(): call(embed_kernel, 'embed', [SMEM(), HBM(), HBM(), HBM(), HBM()], one + o...  9.38 us
    all_to_all x1, waiting for transfers between devices, body(): b_got = lax.all_to_all(b_terms, ('y', 'xhi'), 0, 0)  8.83 us
    ppermute x9, starting transfers between devices, move(): return lax.ppermute(value, AXES, pairs)  7.42 us
    pallas_call x2, Pallas kernels, head_terms(): call(head_pack_kernel, 'head_pack', [VMEM()] * 3, shape((8, 672, 128), BF...  6.89 us
    pallas_call x1, Pallas kernels, body(): call(loss_kernel, 'loss', [SMEM()] + [VMEM()] * 6, shape((1, ROWS), F32))  6.85 us
  transfers between devices with their start and end apart: 11, of which 6 were waited for; matrix products, arithmetic and copies ran while one was open for 9% of the time, Pallas kernels for 31%

profile of v2, /device:TPU:10, one launch (start us, length us, event | category | flops | bytes accessed | tf_op | source)
XLA Modules:
  0.0 130.7 jit_solution(10147214633913657146)
XLA Ops:
  0.6 9.4 %embed.1 = (bf16[512,1152]{1,0:T(8,128)(2,1)S(1)}, f32[512,1152]{1,0:T(8,128)}, f32[512,1]{1,0:T(8,128)}, bf16[512,1152]{1,0:T(8,128)(2,1)}, f32[512,1152]{1,0:T(8,128)}, /*index=5*/f32[512,1]{1,0:T(8,128)}) custom-call(s32[1]{0:T(128)} %bitcast.odd.use_a, bf16[512,1152]{1,0:T(8,128)(2,1)} %image_feats.1, bf16[512,1152]{1,0:T(8,128)(2,1)} %text_feats.1, ...), custom_call_target="tpu_custom_call" | custom-call | flops 1000 | bytes 1000 | tf_op jit(solution)/shard_map/embed/pallas_call | solution.py:93
  12.8 17.6 %conditional.3 = (bf16[512,768]{1,0:T(8,128)(2,1)}, bf16[512,768]{1,0:T(8,128)(2,1)}, bf16[512,768]{1,0:T(8,128)(2,1)S(1)}, bf16[512,768]{1,0:T(8,128)(2,1)}, f32[512,1152]{1,0:T(8,128)}) conditional(s32[]{:T(128)} %convert_element_type.19, () %tuple.34, (s32[]{:T(128)}, bf16[512,1152]{1,0:T(8,128)(2,1)}, bf16[512,1152]{1,0:T(8,128)(2,1)}, s32[]{:T(128)}, ...), branch_computations={%region_0.0_spmd, %region_1.2_spmd} | conditional | flops 3815385856 | bytes 37819152 | solution.py:314
  12.9 4.0 %convolution_convert_fusion.2 = bf16[512,768]{1,0:T(8,128)(2,1)} fusion(bf16[512,1152]{1,0:T(8,128)(2,1)} %get-tuple-element.34, bf16[512,1152]{1,0:T(8,128)(2,1)} %get-tuple-element.50, pred[]{:T(512)S(6)} %eq.14, s32[]{:T(128)S(6)} %mul.17, s32[768]{0:T(1024)S(1)} %get-tuple-element.115, s32[768]{0:T(1024)S(1)} %get-tuple-element.116, ...), kind=kOutput, calls=%fused_computation.40 | convolution fusion | flops 953843712 | bytes 3159557 | tf_op jit(solution)/shard_map/cond/branch_1_fun/dot_general | solution.py:323
  16.9 2.6 %convolution_convert_fusion = bf16[512,768]{1,0:T(8,128)(2,1)} fusion(bf16[512,1152]{1,0:T(8,128)(2,1)S(1)} %copy-done.5, bf16[512,1152]{1,0:T(8,128)(2,1)S(1)} %copy-done.3, pred[]{:T(512)S(6)} %eq.14, s32[]{:T(128)S(6)} %mul.17, s32[768]{0:T(1024)S(1)} %get-tuple-element.115, s32[768]{0:T(1024)S(1)} %get-tuple-element.116, ...), kind=kOutput, calls=%fused_computation.38 | convolution fusion | flops 953843712 | bytes 3159557 | tf_op jit(solution)/shard_map/cond/branch_1_fun/dot_general | solution.py:323
  20.0 3.2 %convolution_convert_fusion.1 = bf16[512,768]{1,0:T(8,128)(2,1)S(1)} fusion(bf16[512,1152]{1,0:T(8,128)(2,1)} %get-tuple-element.50, bf16[512,1152]{1,0:T(8,128)(2,1)} %get-tuple-element.34, pred[]{:T(512)S(6)} %eq.14, s32[]{:T(128)S(6)} %mul.14, s32[768]{0:T(1024)S(1)} %get-tuple-element.115, s32[768]{0:T(1024)S(1)} %get-tuple-element.116, ...), kind=kOutput, calls=%fused_computation.39 | convolution fusion | flops 953843712 | bytes 3159557 | tf_op jit(solution)/shard_map/cond/branch_1_fun/dot_general | solution.py:322
  23.2 2.6 %convolution_convert_fusion.3 = bf16[512,768]{1,0:T(8,128)(2,1)} fusion(bf16[512,1152]{1,0:T(8,128)(2,1)S(1)} %copy-done.4, bf16[512,1152]{1,0:T(8,128)(2,1)S(1)} %copy-done.6, pred[]{:T(512)S(6)} %eq.14, s32[]{:T(128)S(6)} %mul.14, s32[768]{0:T(1024)S(1)} %get-tuple-element.115, s32[768]{0:T(1024)S(1)} %get-tuple-element.116, ...), kind=kOutput, calls=%fused_computation.41 | convolution fusion | flops 953843712 | bytes 3159557 | tf_op jit(solution)/shard_map/cond/branch_1_fun/dot_general | solution.py:322
  25.8 4.6 %side_first.2 = f32[512,1152]{1,0:T(8,128)} custom-call(bf16[512,1152]{1,0:T(8,128)(2,1)S(1)} %get-tuple-element.52.refs_0_, bf16[512,1152]{1,0:T(8,128)(2,1)} %get-tuple-element.53.refs_1_), custom_call_target="tpu_custom_call" | custom-call | flops 1000 | bytes 1000 | tf_op jit(solution)/shard_map/cond/branch_1_fun/side_first/pallas_call | solution.py:150
  30.4 7.7 %collective-permute-done.4.b_from = bf16[512,1152]{1,0:T(8,128)(2,1)} collective-permute-done((bf16[512,1152]{1,0:T(8,128)(2,1)}, bf16[512,1152]{1,0:T(8,128)(2,1)}, u32[]{:S(2)}, u32[]{:S(2)}) %collective-permute-start.4) | collective-permute-done | bytes 1179680 | tf_op jit(solution)/shard_map/ppermute | solution.py:270
  39.8 13.6 %conditional.4 = (bf16[8,672,128]{2,1,0:T(8,128)(2,1)}) conditional(s32[]{:T(128)} %convert_element_type.19, () %tuple.37, (bf16[512,1152]{1,0:T(8,128)(2,1)S(1)}, bf16[512,1152]{1,0:T(8,128)(2,1)}, bf16[512,1152]{1,0:T(8,128)(2,1)}, f32[512,1152]{1,0:T(8,128)}, f32[512,1152]{1,0:T(8,128)}, /*index=5*/f32[512,1]{1,0:T(8,128)}, ...), branch_computations={%region_2.3_spmd, %region_3.4_spmd} | conditional | flops 3000 | bytes 4721640 | solution.py:314
  39.8 7.2 %side_last.2.grad = bf16[1152,512]{1,0:T(8,128)(2,1)S(1)} custom-call(bf16[512,1152]{1,0:T(8,128)(2,1)S(1)} %get-tuple-element.54.refs_0_, bf16[512,1152]{1,0:T(8,128)(2,1)} %get-tuple-element.55.refs_1_, bf16[512,1152]{1,0:T(8,128)(2,1)} %get-tuple-element.56.refs_2_, f32[512,1152]{1,0:T(8,128)} %get-tuple-element.57.refs_3_, ...), custom_call_target="tpu_custom_call" | custom-call | flops 1000 | bytes 1000 | tf_op jit(solution)/shard_map/cond/branch_1_fun/side_last/pallas_call | solution.py:150
  47.1 2.2 %head_own.2.before = f32[1152,768]{1,0:T(8,128)S(1)} custom-call(bf16[1152,512]{1,0:T(8,128)(2,1)S(1)} %side_last.2.grad, bf16[512,768]{1,0:T(8,128)(2,1)} %get-tuple-element.61.feats), custom_call_target="tpu_custom_call" | custom-call | flops 1000 | bytes 1000 | tf_op jit(solution)/shard_map/cond/branch_1_fun/head_own/pallas_call | solution.py:334
  50.0 3.5 %head_pack.2 = bf16[8,672,128]{2,1,0:T(8,128)(2,1)} custom-call(bf16[1152,512]{1,0:T(8,128)(2,1)S(1)} %collective-permute-done.grad, bf16[512,768]{1,0:T(8,128)(2,1)} %get-tuple-element.60.feats, f32[1152,768]{1,0:T(8,128)S(1)} %head_own.2.before), custom_call_target="tpu_custom_call" | custom-call | flops 1000 | bytes 1000 | tf_op jit(solution)/shard_map/cond/branch_1_fun/head_pack/pallas_call | solution.py:335
  53.4 6.5 %all-to-all-start = ((bf16[4,2,672,128]{3,2,1,0:T(8,128)(2,1)}), bf16[4,2,672,128]{3,2,1,0:T(8,128)(2,1)S(1)}, u32[]{:S(2)}, u32[]{:S(2)}) async-start(bf16[4,2,672,128]{3,2,1,0:T(8,128)(2,1)} %bitcast.3), calls=%async_computation | async-start | bytes 2752512 | tf_op jit(solution)/shard_map/all_to_all | solution.py:341
  59.9 6.4 %side_first.3 = f32[512,1152]{1,0:T(8,128)} custom-call(bf16[512,1152]{1,0:T(8,128)(2,1)} %get-tuple-element.94.refs_0_.b_emb, bf16[512,1152]{1,0:T(8,128)(2,1)} %copy-done.2, bf16[512,1152]{1,0:T(8,128)(2,1)S(1)} %collective-permute-done.5.refs_2_.a_from), custom_call_target="tpu_custom_call" | custom-call | flops 1000 | bytes 1000 | tf_op jit(solution)/shard_map/side_first/pallas_call | solution.py:150
  66.3 12.1 %conditional.5 = (bf16[8,672,128]{2,1,0:T(8,128)(2,1)}) conditional(s32[]{:T(128)} %convert_element_type.19, () %tuple.33, (bf16[512,1152]{1,0:T(8,128)(2,1)}, bf16[512,1152]{1,0:T(8,128)(2,1)}, f32[512,1152]{1,0:T(8,128)}, f32[512,1152]{1,0:T(8,128)}, f32[512,1]{1,0:T(8,128)}, /*index=5*/bf16[512,768]{1,0:T(8,128)(2,1)S(1)}, ...), branch_computations={%region_4.5_spmd, %region_5.6_spmd} | conditional | flops 3000 | bytes 4721640 | solution.py:314
  66.3 5.5 %side_last.3.grad = bf16[1152,512]{1,0:T(8,128)(2,1)S(1)} custom-call(bf16[512,1152]{1,0:T(8,128)(2,1)} %get-tuple-element.62.refs_0_, bf16[512,1152]{1,0:T(8,128)(2,1)} %get-tuple-element.63.refs_1_, f32[512,1152]{1,0:T(8,128)} %get-tuple-element.64.refs_2_, f32[512,1152]{1,0:T(8,128)} %get-tuple-element.65.refs_3_, f32[512,1]{1,0:T(8,128)} %get-tuple-element.66.refs_4_), custom_call_target="tpu_custom_call" | custom-call | flops 1000 | bytes 1000 | tf_op jit(solution)/shard_map/cond/branch_1_fun/side_last/pallas_call | solution.py:150
  73.2 1.7 %collective-permute-done.1.grad = bf16[1152,512]{1,0:T(8,128)(2,1)S(1)} collective-permute-done((bf16[1152,512]{1,0:T(8,128)(2,1)S(1)}, bf16[1152,512]{1,0:T(8,128)(2,1)S(1)}, u32[]{:S(2)}, u32[]{:S(2)}) %collective-permute-start.1) | collective-permute-done | bytes 1179680 | tf_op jit(solution)/shard_map/cond/branch_1_fun/ppermute | solution.py:270
  74.9 3.4 %head_pack.3 = bf16[8,672,128]{2,1,0:T(8,128)(2,1)} custom-call(bf16[1152,512]{1,0:T(8,128)(2,1)S(1)} %collective-permute-done.1.grad, bf16[512,768]{1,0:T(8,128)(2,1)} %get-tuple-element.67.feats, f32[1152,768]{1,0:T(8,128)S(1)} %head_own.3.before), custom_call_target="tpu_custom_call" | custom-call | flops 1000 | bytes 1000 | tf_op jit(solution)/shard_map/cond/branch_1_fun/head_pack/pallas_call | solution.py:335
  78.4 6.7 %all-to-all-start.1 = ((bf16[8,672,128]{2,1,0:T(8,128)(2,1)}), bf16[8,672,128]{2,1,0:T(8,128)(2,1)S(1)}, u32[]{:S(2)}, u32[]{:S(2)}) async-start(bf16[8,672,128]{2,1,0:T(8,128)(2,1)} %get-tuple-element.131), calls=%async_computation.1 | async-start | bytes 2752512 | tf_op jit(solution)/shard_map/all_to_all | solution.py:352
  85.2 3.1 %collective-permute-start.8 = (bf16[672,128]{1,0:T(8,128)(2,1)S(1)}, bf16[672,128]{1,0:T(8,128)(2,1)S(1)}, u32[]{:S(2)}, u32[]{:S(2)}) collective-permute-start(bf16[672,128]{1,0:T(8,128)(2,1)S(1)} %get-tuple-element.110), channel_id=1, source_target_pairs={{0,16},{1,17},{2,18},{3,19},{4,20},{5,21},{6,22},{7,23},{8,24},{9,... | collective-permute-start | bytes 516104 | tf_op jit(solution)/shard_map/ppermute | solution.py:270
  89.5 6.9 %loss.1 = f32[1,512]{1,0:T(1,128)} custom-call(s32[1]{0:T(128)} %bitcast.odd.use_a, bf16[512,1152]{1,0:T(8,128)(2,1)} %copy-done.2, bf16[512,1152]{1,0:T(8,128)(2,1)} %get-tuple-element.94.refs_0_.b_emb, bf16[512,1152]{1,0:T(8,128)(2,1)} %collective-permute-done.7.a_cross, bf16[512,1152]{1,0:T(8,128)(2,1)} %collective-permute-done.6.b_cross, ...), custom_call_target="tpu_custom_call" | custom-call | flops 1000 | bytes 1000 | tf_op jit(solution)/shard_map/loss/pallas_call | solution.py:355
  96.4 8.8 %all-to-all-done.1.b_got = bf16[8,672,128]{2,1,0:T(8,128)(2,1)S(1)} async-done(((bf16[8,672,128]{2,1,0:T(8,128)(2,1)}), bf16[8,672,128]{2,1,0:T(8,128)(2,1)S(1)}, u32[]{:S(2)}, u32[]{:S(2)}) %all-to-all-start.1) | async-done | bytes 1376288 | tf_op jit(solution)/shard_map/all_to_all | solution.py:352
  105.2 1.9 %collective-permute-done.8.a_take = bf16[672,128]{1,0:T(8,128)(2,1)S(1)} collective-permute-done((bf16[672,128]{1,0:T(8,128)(2,1)S(1)}, bf16[672,128]{1,0:T(8,128)(2,1)S(1)}, u32[]{:S(2)}, u32[]{:S(2)}) %collective-permute-start.8) | collective-permute-done | bytes 172064 | tf_op jit(solution)/shard_map/ppermute | solution.py:270
  107.8 22.1 %all_to_all.15 = bf16[16,2,48,128]{3,2,1,0:T(8,128)(2,1)S(1)} all-to-all(bf16[16,2,48,128]{3,2,1,0:T(8,128)(2,1)S(1)} %bitcast.6), channel_id=1, replica_groups=mesh['y'=4,'xlo'=2,'xhi'=2,'z'=8,'core'=2] {'z','xlo'}, dimensions={0} | all-to-all | bytes 786432 | tf_op jit(solution)/shard_map/all_to_all | solution.py:360
  (36 shorter events, 10.0 us)
Async XLA Ops:
  10.0 29.8 %copy-start.2 = (bf16[512,1152]{1,0:T(8,128)(2,1)}, bf16[512,1152]{1,0:T(8,128)(2,1)S(1)}, u32[]{:S(2)}) copy-start(bf16[512,1152]{1,0:T(8,128)(2,1)S(1)} %get-tuple-element.108.refs_1_.a_emb) | copy-start | bytes 3538948
  10.0 28.1 %collective-permute-start.4 = (bf16[512,1152]{1,0:T(8,128)(2,1)}, bf16[512,1152]{1,0:T(8,128)(2,1)}, u32[]{:S(2)}, u32[]{:S(2)}) collective-permute-start(bf16[512,1152]{1,0:T(8,128)(2,1)} %get-tuple-element.94.refs_0_.b_emb), channel_id=1, source_target_pairs={{0,192},{1,193},{2,194},{3,195},{4,196},{5,197},{6,198},{7,199},{8... | collective-permute-start | bytes 3538952 | tf_op jit(solution)/shard_map/ppermute | solution.py:270
  11.7 27.4 %collective-permute-start.5 = (bf16[512,1152]{1,0:T(8,128)(2,1)S(1)}, bf16[512,1152]{1,0:T(8,128)(2,1)S(1)}, u32[]{:S(2)}, u32[]{:S(2)}) collective-permute-start(bf16[512,1152]{1,0:T(8,128)(2,1)S(1)} %get-tuple-element.108.refs_1_.a_emb), channel_id=1, source_target_pairs={{0,64},{1,65},{2,66},{3,67},{4,68},{5,69},{6,70},{7,71},{8,72},{9,... | collective-permute-start | bytes 3538952 | tf_op jit(solution)/shard_map/ppermute | solution.py:270
  12.1 27.7 %collective-permute-start.7 = (bf16[512,1152]{1,0:T(8,128)(2,1)S(1)}, bf16[512,1152]{1,0:T(8,128)(2,1)}, u32[]{:S(2)}, u32[]{:S(2)}) collective-permute-start(bf16[512,1152]{1,0:T(8,128)(2,1)S(1)} %get-tuple-element.108.refs_1_.a_emb), channel_id=1, source_target_pairs={{0,32},{1,33},{2,34},{3,35},{4,36},{5,37},{6,38},{7,39},{8,40},{9,... | collective-permute-start | bytes 3538952 | tf_op jit(solution)/shard_map/ppermute | solution.py:270
  12.9 4.0 %copy-start.3 = (bf16[512,1152]{1,0:T(8,128)(2,1)S(1)}, bf16[512,1152]{1,0:T(8,128)(2,1)}, u32[]{:S(2)}) copy-start(bf16[512,1152]{1,0:T(8,128)(2,1)} %get-tuple-element.34) | copy-start | bytes 3538948 | tf_op jit(solution)/shard_map/cond
  12.9 4.0 %copy-start.5 = (bf16[512,1152]{1,0:T(8,128)(2,1)S(1)}, bf16[512,1152]{1,0:T(8,128)(2,1)}, u32[]{:S(2)}) copy-start(bf16[512,1152]{1,0:T(8,128)(2,1)} %get-tuple-element.50) | copy-start | bytes 3538948 | tf_op jit(solution)/shard_map/cond
  16.9 13.5 %collective-permute-start.2 = (bf16[512,768]{1,0:T(8,128)(2,1)}, bf16[512,768]{1,0:T(8,128)(2,1)}, u32[]{:S(2)}, u32[]{:S(2)}) collective-permute-start(bf16[512,768]{1,0:T(8,128)(2,1)} %convolution_convert_fusion.2), channel_id=1, source_target_pairs={{0,1},{1,0},{2,3},{3,2},{4,5},{5,4},{6,7},{7,6},{8,9},{9,8},{10,11... | collective-permute-start | bytes 2359304 | tf_op jit(solution)/shard_map/cond/branch_1_fun/ppermute | solution.py:270
  19.5 10.9 %collective-permute-start.3 = (bf16[512,768]{1,0:T(8,128)(2,1)}, bf16[512,768]{1,0:T(8,128)(2,1)}, u32[]{:S(2)}, u32[]{:S(2)}) collective-permute-start(bf16[512,768]{1,0:T(8,128)(2,1)} %convolution_convert_fusion), channel_id=1, source_target_pairs={{0,1},{1,0},{2,3},{3,2},{4,5},{5,4},{6,7},{7,6},{8,9},{9,8},{10,11... | collective-permute-start | bytes 2359304 | tf_op jit(solution)/shard_map/cond/branch_1_fun/ppermute | solution.py:270
  20.0 3.2 %copy-start.4 = (bf16[512,1152]{1,0:T(8,128)(2,1)S(1)}, bf16[512,1152]{1,0:T(8,128)(2,1)}, u32[]{:S(2)}) copy-start(bf16[512,1152]{1,0:T(8,128)(2,1)} %get-tuple-element.34) | copy-start | bytes 3538948 | tf_op jit(solution)/shard_map/cond
  20.0 3.2 %copy-start.6 = (bf16[512,1152]{1,0:T(8,128)(2,1)S(1)}, bf16[512,1152]{1,0:T(8,128)(2,1)}, u32[]{:S(2)}) copy-start(bf16[512,1152]{1,0:T(8,128)(2,1)} %get-tuple-element.50) | copy-start | bytes 3538948 | tf_op jit(solution)/shard_map/cond
  39.1 20.8 %copy-start = (bf16[512,1152]{1,0:T(8,128)(2,1)}, bf16[512,1152]{1,0:T(8,128)(2,1)S(1)}, u32[]{:S(2)}) copy-start(bf16[512,1152]{1,0:T(8,128)(2,1)S(1)} %collective-permute-done.5.refs_2_.a_from) | copy-start | bytes 3538948
  39.1 27.1 %collective-permute-start.6 = (bf16[512,1152]{1,0:T(8,128)(2,1)}, bf16[512,1152]{1,0:T(8,128)(2,1)}, u32[]{:S(2)}, u32[]{:S(2)}) collective-permute-start(bf16[512,1152]{1,0:T(8,128)(2,1)} %collective-permute-done.4.b_from), channel_id=1, source_target_pairs={{0,32},{1,33},{2,34},{3,35},{4,36},{5,37},{6,38},{7,39},{8,40},{9,... | collective-permute-start | bytes 3538952 | tf_op jit(solution)/shard_map/ppermute | solution.py:270
  47.0 2.9 %collective-permute-start = (bf16[1152,512]{1,0:T(8,128)(2,1)S(1)}, bf16[1152,512]{1,0:T(8,128)(2,1)S(1)}, u32[]{:S(2)}, u32[]{:S(2)}) collective-permute-start(bf16[1152,512]{1,0:T(8,128)(2,1)S(1)} %side_last.2.grad), channel_id=1, source_target_pairs={{0,1},{1,0},{2,3},{3,2},{4,5},{5,4},{6,7},{7,6},{8,9},{9,8},{10,11... | collective-permute-start | bytes 3538952 | tf_op jit(solution)/shard_map/cond/branch_1_fun/ppermute | solution.py:270
  53.4 24.9 %all-to-all-start = ((bf16[4,2,672,128]{3,2,1,0:T(8,128)(2,1)}), bf16[4,2,672,128]{3,2,1,0:T(8,128)(2,1)S(1)}, u32[]{:S(2)}, u32[]{:S(2)}) async-start(bf16[4,2,672,128]{3,2,1,0:T(8,128)(2,1)} %bitcast.3), calls=%async_computation | async-start | bytes 2752512 | tf_op jit(solution)/shard_map/all_to_all | solution.py:341
  71.8 3.2 %collective-permute-start.1 = (bf16[1152,512]{1,0:T(8,128)(2,1)S(1)}, bf16[1152,512]{1,0:T(8,128)(2,1)S(1)}, u32[]{:S(2)}, u32[]{:S(2)}) collective-permute-start(bf16[1152,512]{1,0:T(8,128)(2,1)S(1)} %side_last.3.grad), channel_id=1, source_target_pairs={{0,1},{1,0},{2,3},{3,2},{4,5},{5,4},{6,7},{7,6},{8,9},{9,8},{10,11... | collective-permute-start | bytes 3538952 | tf_op jit(solution)/shard_map/cond/branch_1_fun/ppermute | solution.py:270
  78.4 26.8 %all-to-all-start.1 = ((bf16[8,672,128]{2,1,0:T(8,128)(2,1)}), bf16[8,672,128]{2,1,0:T(8,128)(2,1)S(1)}, u32[]{:S(2)}, u32[]{:S(2)}) async-start(bf16[8,672,128]{2,1,0:T(8,128)(2,1)} %get-tuple-element.131), calls=%async_computation.1 | async-start | bytes 2752512 | tf_op jit(solution)/shard_map/all_to_all | solution.py:352
  85.2 21.9 %collective-permute-start.8 = (bf16[672,128]{1,0:T(8,128)(2,1)S(1)}, bf16[672,128]{1,0:T(8,128)(2,1)S(1)}, u32[]{:S(2)}, u32[]{:S(2)}) collective-permute-start(bf16[672,128]{1,0:T(8,128)(2,1)S(1)} %get-tuple-element.110), channel_id=1, source_target_pairs={{0,16},{1,17},{2,18},{3,19},{4,20},{5,21},{6,22},{7,23},{8,24},{9,... | collective-permute-start | bytes 516104 | tf_op jit(solution)/shard_map/ppermute | solution.py:270
  88.2 1.3 copy-start.1

commit v3 on v2

--- a/solution.py
+++ b/solution.py
@@ -49,13 +49,11 @@
 
 def embed_kernel(odd, image_feats, text_feats, image_head, text_head, *refs):
     outs, (feats, head, held, in_sems, out_sems) = refs[:6], refs[6:]
-    cut = 3
-    width = D // cut
+    cuts = (pl.ds(0, 512), pl.ds(512, 512), pl.ds(1024, 128))
 
     def loads(side, src_feats, src_head):
-        yield pltpu.make_async_copy(src_feats, feats.at[side], in_sems.at[side, cut])
-        for j in range(cut):
-            cols = pl.ds(j * width, width)
+        yield pltpu.make_async_copy(src_feats, feats.at[side], in_sems.at[side, 3])
+        for j, cols in enumerate(cuts):
             yield pltpu.make_async_copy(src_head.at[:, cols], head.at[side, :, cols], in_sems.at[side, j])
 
     for value in range(2):
@@ -73,8 +71,7 @@
         waits = list(loads(side, image_feats, image_head))
         waits[0].wait()
         total = jnp.zeros((ROWS, 1), F32)
-        for j in range(cut):
-            cols = pl.ds(j * width, width)
+        for j, cols in enumerate(cuts):
             waits[j + 1].wait()
             proj = jnp.dot(feats[side], head[side, :, cols], preferred_element_type=F32)
             held[side, :, cols] = proj
@@ -120,39 +117,69 @@
     return jnp.dot(weights.astype(BF16), theirs[...], preferred_element_type=F32)
 
 
-def side_kernel(count, diagonal, last, *refs):
-    mine, partners, rest = refs[0], refs[1 : 1 + count], refs[1 + count :]
-    if last:
-        before, proj, norm, out = rest
-    else:
-        (out,) = rest
+def side_kernel(count, diagonal, adds, last, *refs):
+    refs = list(refs)
+    take = lambda number: [refs.pop(0) for _ in range(number)]
+    sources = take(1 + count + adds + last)
+    norm = take(1)[0] if last else None
+    (out,) = take(1)
+    bufs = take(len(sources))
+    held = None if last else take(1)[0]
+    in_sems, out_sems = refs
     block = 256
-    for i in range(ROWS // block):
-        rows = pl.ds(i * block, block)
-        grad = before[rows, :] if last else None
-        for step, theirs in enumerate(partners):
-            part = add_pair(mine, theirs, rows, diagonal and step == 0)
+    parts = [pl.ds(i * block, block) for i in range(ROWS // block)]
+    loads = {}
+    for k in range(1 + count):
+        loads[k] = pltpu.make_async_copy(sources[k], bufs[k], in_sems.at[k, 0])
+        loads[k].start()
+    for i, rows in enumerate(parts):
+        for k in range(1 + count, len(sources)):
+            loads[k, i] = pltpu.make_async_copy(sources[k].at[rows, :], bufs[k].at[rows, :], in_sems.at[k, i])
+            loads[k, i].start()
+    saves = []
+    loads[0].wait()
+    for i, rows in enumerate(parts):
+        grad = None
+        for step in range(count):
+            if i == 0:
+                loads[1 + step].wait()
+            part = add_pair(bufs[0], bufs[1 + step], rows, diagonal and step == 0)
             grad = part if grad is None else grad + part
+        if adds:
+            loads[1 + count, i].wait()
+            grad = grad + bufs[1 + count][rows, :]
         if last:
+            loads[1 + count + adds, i].wait()
             grad = TEMP * grad
             inverse = 1.0 / norm[rows, :]
-            own = proj[rows, :] * inverse
+            own = bufs[1 + count + adds][rows, :] * inverse
             along = jnp.sum(own * grad, axis=1, keepdims=True)
             value = (grad - own * along) * inverse
-            out[:, rows] = value.T.astype(BF16)
+            out[:, rows] = value.astype(BF16).T
         else:
-            out[rows, :] = grad
+            held[rows, :] = grad
+            saves.append(pltpu.make_async_copy(held.at[rows, :], out.at[rows, :], out_sems.at[i]))
+            saves[-1].start()
+    for copy in saves:
+        copy.wait()
 
 
 def side(mine, partners, diagonal, before=None, proj=None, norm=None):
-    last = before is not None
-    args = [mine, *partners] + ([before, proj, norm] if last else [])
+    last = proj is not None
+    adds = before is not None
+    args = [mine, *partners] + [before] * adds + [proj] * last
+    wide = pltpu.VMEM((ROWS, D), F32)
+    scratch = [pltpu.VMEM((ROWS, D), BF16)] * (1 + len(partners)) + [wide] * (adds + last) + [wide] * (not last)
+    scratch += [pltpu.SemaphoreType.DMA((len(args), 2)), pltpu.SemaphoreType.DMA((2,))]
     return call(
-        functools.partial(side_kernel, len(partners), diagonal, last),
+        functools.partial(side_kernel, len(partners), diagonal, adds, last),
         "side_last" if last else "side_first",
-        [VMEM()] * len(args),
+        [HBM()] * len(args) + [VMEM()] * last,
         shape((D, ROWS), BF16) if last else shape((ROWS, D), F32),
-    )(*args)
+        out_specs=VMEM() if last else HBM(),
+        scratch=scratch,
+        vmem=24,
+    )(*args, *([norm] * last))
 
 
 def loss_kernel(use_a, a_emb, b_emb, a_cross, b_cross, a_from, b_from, out):
@@ -182,70 +209,73 @@
     out[...] = jnp.dot(grad[...], feats[...], preferred_element_type=F32)
 
 
-def head_pack_kernel(grad, feats, before, out):
+def head_pack_kernel(grad, feats, before, out, held, sems):
+    copies = []
     for y in range(4):
         rows = pl.ds(y * 288, 288)
         terms = before[rows, :] + jnp.dot(grad[rows, :], feats[...], preferred_element_type=F32)
-        for xhi in range(2):
-            base = xhi * 384
-            chunk = 2 * y + xhi
-            out[chunk, 0:288, :] = terms[:, base : base + 128].astype(BF16)
-            out[chunk, 288:576, :] = terms[:, base + 128 : base + 256].astype(BF16)
-            few = terms[:, base + 256 : base + 384]
-            few = few[0:96] + pltpu.roll(few[96:192], 32, 1) + pltpu.roll(few[192:288], 64, 1)
-            out[chunk, 576:672, :] = few.astype(BF16)
+        for xlo in range(2):
+            for xhi in range(2):
+                some = terms[xlo * 144 : xlo * 144 + 144, xhi * 384 : xhi * 384 + 384]
+                chunk = 4 * y + 2 * xlo + xhi
+                held[chunk, 0:144, :] = some[:, 0:128].astype(BF16)
+                held[chunk, 144:288, :] = some[:, 128:256].astype(BF16)
+                few = some[:, 256:384]
+                few = few[0:48] + pltpu.roll(few[48:96], 32, 1) + pltpu.roll(few[96:144], 64, 1)
+                held[chunk, 288:336, :] = few.astype(BF16)
+        four = pl.ds(4 * y, 4)
+        copies.append(pltpu.make_async_copy(held.at[four], out.at[four], sems.at[y]))
+        copies[-1].start()
+    for copy in copies:
+        copy.wait()
 
 
 def repack(total, store):
     lane = lax.broadcasted_iota(jnp.int32, (48, 128), 1)
     for z in range(8):
-        for xlo in range(2):
-            value = jnp.zeros((48, 128), F32)
-            for g in range(3):
-                m = xlo * 144 + g * 48
-                wide = total[(z // 4) * 288 + m : (z // 4) * 288 + m + 48, :]
-                move = (32 * g - 32 * (z % 4)) % 128
-                wide = pltpu.roll(wide, move, 1) if move else wide
-                value = jnp.where((lane >= 32 * g) & (lane < 32 * g + 32), wide, value)
-                group, row = m // 96, m % 96
-                few = total[576 + row : 576 + row + 48, :]
-                move = (96 + 4 * g - 32 * group - 4 * z) % 128
-                few = pltpu.roll(few, move, 1) if move else few
-                first = 96 + 4 * g
-                value = jnp.where((lane >= first) & (lane < first + 4), few, value)
-            store(z, xlo, value)
-
-
-def add_y_kernel(xhi, got, keep, give):
-    def total(which):
+        value = jnp.zeros((48, 128), F32)
+        for g in range(3):
+            first = (z // 4) * 144 + g * 48
+            wide = total[first : first + 48, :]
+            turn = (32 * g - 32 * (z % 4)) % 128
+            wide = pltpu.roll(wide, turn, 1) if turn else wide
+            value = jnp.where((lane >= 32 * g) & (lane < 32 * g + 32), wide, value)
+            few = total[288:336, :]
+            turn = (96 + 4 * g - 32 * g - 4 * z) % 128
+            few = pltpu.roll(few, turn, 1) if turn else few
+            first = 96 + 4 * g
+            value = jnp.where((lane >= first) & (lane < first + 4), few, value)
+        store(z, value)
+
+
+def add_y_kernel(me, got, *outs):
+    for far, out in enumerate(outs):
+        which = me[0] ^ far
         value = got[0, which].astype(F32)
         for s in range(1, 4):
             value = value + got[s, which].astype(F32)
-        return value
-
-    keep[...] = total(xhi[0])
-    give[...] = total(1 - xhi[0]).astype(BF16)
-
-
-def add_pack_kernel(a_keep, a_take, b_got, out):
-    a_total = a_keep[...] + a_take[...].astype(F32)
-    b_total = b_got[0].astype(F32)
-    for s in range(1, 8):
-        b_total = b_total + b_got[s].astype(F32)
-    for side, total in enumerate((a_total, b_total)):
-
-        def store(z, xlo, value, side=side):
-            out[z, xlo, side] = value.astype(BF16)
+        out[...] = value.astype(out.dtype)
+
+
+def add_pack_kernel(odd, keep, near, cross, corner, b_got, out):
+    same = keep[...] + near[...].astype(F32)
+    other = cross[...].astype(F32) + corner[...].astype(F32)
+    is_odd = odd[0] == 1
+    for head in range(2):
+        total = jnp.where(is_odd, other, same) if head == 0 else jnp.where(is_odd, same, other)
+        for y in range(4):
+            for xhi in range(2):
+                total = total + b_got[4 * y + 2 * (1 - head) + xhi].astype(F32)
+
+        def store(z, value, head=head):
+            out[z, head] = value
 
         repack(total, store)
 
 
-def finish_kernel(got, image, text):
-    for out, parity in ((text, 0), (image, 1)):
-        value = jnp.zeros((48, 128), F32)
-        for z in range(8):
-            value = value + got[z, parity, 0].astype(F32) + got[z, 1 - parity, 1].astype(F32)
-        turned = value.T
+def finish_kernel(got, text, image):
+    for head, out in enumerate((text, image)):
+        turned = jnp.sum(got[:, head], axis=0).T
         parts = []
         for g in range(3):
             parts.append(jnp.concatenate([turned[32 * g : 32 * g + 32], turned[96 + 4 * g : 100 + 4 * g]], axis=0))
@@ -323,44 +353,55 @@
             oth = jnp.dot(feats, oth_columns, preferred_element_type=F32).astype(BF16)
             return own, swap_core(oth)
 
-        return (*columns(a_feats), *columns(b_feats), side(a_emb, (b_emb,), True))
-
-    a_own, a_oth, b_own, b_oth, a_first = together(prepare, image_feats, text_feats, a_emb, b_emb)
-    b_from, a_from = after((b_from, a_from), a_own, b_own, a_oth, b_oth, a_first)
+        firsts = side(a_emb, (b_emb,), True), side(b_emb, (a_emb,), True)
+        return (*columns(a_feats), *columns(b_feats), *firsts)
+
+    a_own, a_oth, b_own, b_oth, a_first, b_first = together(prepare, image_feats, text_feats, a_emb, b_emb)
+    (a_cross,) = after((a_cross,), a_own, b_own, a_oth, b_oth, a_first, b_first)
+    (b_from,) = after((b_from,), a_cross)
     b_cross = swap_x(b_from)
+    (a_first,) = after((a_first,), a_from)
 
     def head_terms(mine, own, oth):
         theirs = swap_core(mine)
         before = call(head_own_kernel, "head_own", [VMEM()] * 2, shape((D, 768), F32))(mine, own)
-        return call(head_pack_kernel, "head_pack", [VMEM()] * 3, shape((8, 672, 128), BF16))(theirs, oth, before)
+        return call(
+            head_pack_kernel,
+            "head_pack",
+            [VMEM()] * 3,
+            shape((16, 336, 128), BF16),
+            out_specs=HBM(),
+            scratch=[pltpu.VMEM((16, 336, 128), BF16), pltpu.SemaphoreType.DMA((4,))],
+        )(theirs, oth, before)
 
     def finished(mine, partners, before, proj, norm, own, oth):
         return head_terms(side(mine, partners, False, before, proj, norm), own, oth)
 
     a_terms = together(finished, a_emb, (a_cross, b_from), a_first, a_proj, a_norm, a_own, a_oth)
-    a_got = lax.all_to_all(a_terms.reshape(4, 2, 672, 128), "y", 0, 0)
+    a_got = lax.all_to_all(a_terms.reshape(4, 4, 336, 128), "y", 0, 0)
+    me = (2 * odd + lax.axis_index("xhi")).astype(jnp.int32).reshape(1)
+    keep, near, cross, corner = call(add_y_kernel, "add_y", [SMEM(), VMEM()], [shape((336, 128), F32)] + [shape((336, 128), BF16)] * 3)(
+        me, a_got
+    )
+    near = move(near, lambda y, xl, xh, z, c: (y, xl, 1 - xh, z, c))
+    cross = move(cross, lambda y, xl, xh, z, c: (y, 1 - xl, xh, z, c))
+    corner = move(corner, lambda y, xl, xh, z, c: (y, 1 - xl, 1 - xh, z, c))
 
     (a_from,) = after((a_from,), a_terms)
-    b_first = side(b_emb, (a_emb, a_from), True)
-    a_keep, a_give = call(
-        add_y_kernel, "add_y", [SMEM(), VMEM()], [shape((672, 128), F32), shape((672, 128), BF16)]
-    )(lax.axis_index("xhi").astype(jnp.int32).reshape(1), a_got)
-    a_take = move(a_give, lambda y, xl, xh, z, c: (y, xl, 1 - xh, z, c))
-
-    (b_cross,) = after((b_cross,), b_first)
+    b_first = side(b_emb, (a_from,), False, b_first)
     b_terms = together(finished, b_emb, (b_cross,), b_first, b_proj, b_norm, b_own, b_oth)
-    b_got = lax.all_to_all(b_terms, ("y", "xhi"), 0, 0)
+    b_got = lax.all_to_all(b_terms, ("y", "xlo", "xhi"), 0, 0)
 
     (loss_emb,) = after((a_emb,), b_terms)
     row_loss = call(loss_kernel, "loss", [SMEM()] + [VMEM()] * 6, shape((1, ROWS), F32))(
         flag, loss_emb, b_emb, a_cross, b_cross, a_from, b_from
     )
     (b_got,) = after((b_got,), row_loss)
-    part = call(add_pack_kernel, "add_pack", [VMEM()] * 3, shape((8, 2, 2, 48, 128), BF16))(a_keep, a_take, b_got)
-    got = lax.all_to_all(part.reshape(16, 2, 48, 128), ("z", "xlo"), 0, 0).reshape(8, 2, 2, 48, 128)
-    image_grad, text_grad = call(
-        finish_kernel, "finish", [VMEM()], [shape((36, 144), F32), shape((36, 144), F32)]
-    )(got)
+    part = call(add_pack_kernel, "add_pack", [SMEM()] + [VMEM()] * 5, shape((8, 2, 48, 128), F32))(
+        flag, keep, near, cross, corner, b_got
+    )
+    got = lax.all_to_all(part, "z", 0, 0)
+    text_grad, image_grad = call(finish_kernel, "finish", [VMEM()], [shape((36, 144), F32), shape((36, 144), F32)])(got)
     return row_loss.reshape(ROWS), image_grad, text_grad
 
 

time: 133 us -> 130 us (0.977)
  waiting for transfers between devices: 21.8 us -> 17.6 us
  starting transfers between devices: 20.5 us -> 23.4 us
    ppermute x9 -> x11, waiting for transfers between devices: 13 us -> 8.2 us  [move(): return lax.ppermute(value, AXES, pairs)]
    ppermute x9 -> x11, starting transfers between devices: 7.42 us -> 9.16 us  [move(): return lax.ppermute(value, AXES, pairs)]
    pallas_call x8 -> x9, Pallas kernels: 31.4 us -> 32 us  [the longest x5 25.1 us: side(): call(functools.partial(side_kernel, len(partners), diagonal, adds, last),...]
  transfers between devices with their start and end apart: 11 -> 13, of which waited for: 6 -> 8; matrix products, arithmetic and copies ran while one was open for 9% -> 10% of each run, Pallas kernels for 31% -> 32%
where the time goes in v3:
time: 130 us; the launch traced here: 129 us
  Pallas kernels  52.2 us (40%)
  starting transfers between devices  23.4 us (18%)
  blocking collectives  21.2 us (16%)
  waiting for transfers between devices  17.6 us (14%)
  matrix products  12.4 us (10%)
  local copies, waits for them, and re-layouts  1.3 us (1%)
    pallas_call x5, Pallas kernels, side(): call(functools.partial(side_kernel, len(partners), diagonal, adds, last),...  25.1 us
    all_to_all x1, blocking collectives, body(): got = lax.all_to_all(part, 'z', 0, 0)  21.2 us
    ppermute x11, starting transfers between devices, move(): return lax.ppermute(value, AXES, pairs)  9.16 us
    pallas_call x1, Pallas kernels, embed(): call(embed_kernel, 'embed', [SMEM(), HBM(), HBM(), HBM(), HBM()], one + o...  8.99 us
    all_to_all x1, waiting for transfers between devices, body(): b_got = lax.all_to_all(b_terms, ('y', 'xlo', 'xhi'), 0, 0)  8.47 us
    all_to_all x1, starting transfers between devices, body(): b_got = lax.all_to_all(b_terms, ('y', 'xlo', 'xhi'), 0, 0)  8.3 us
    ppermute x11, waiting for transfers between devices, move(): return lax.ppermute(value, AXES, pairs)  8.2 us
    pallas_call x1, Pallas kernels, body(): call(loss_kernel, 'loss', [SMEM()] + [VMEM()] * 6, shape((1, ROWS), F32))  7.1 us
  transfers between devices with their start and end apart: 13, of which 8 were waited for; matrix products, arithmetic and copies ran while one was open for 10% of the time, Pallas kernels for 32%

profile of v3, /device:TPU:10, one launch (start us, length us, event | category | flops | bytes accessed | tf_op | source)
XLA Modules:
  0.0 129.0 jit_solution(15746820511421048700)
XLA Ops:
  0.6 9.0 %embed.1 = (bf16[512,1152]{1,0:T(8,128)(2,1)S(1)}, f32[512,1152]{1,0:T(8,128)}, f32[512,1]{1,0:T(8,128)}, bf16[512,1152]{1,0:T(8,128)(2,1)}, f32[512,1152]{1,0:T(8,128)}, /*index=5*/f32[512,1]{1,0:T(8,128)}) custom-call(s32[1]{0:T(128)} %bitcast.odd.use_a, bf16[512,1152]{1,0:T(8,128)(2,1)} %image_feats.1, bf16[512,1152]{1,0:T(8,128)(2,1)} %text_feats.1, ...), custom_call_target="tpu_custom_call" | custom-call | flops 1000 | bytes 1000 | tf_op jit(solution)/shard_map/embed/pallas_call | solution.py:90
  10.3 1.6 %collective-permute-start.4 = (bf16[512,1152]{1,0:T(8,128)(2,1)}, bf16[512,1152]{1,0:T(8,128)(2,1)}, u32[]{:S(2)}, u32[]{:S(2)}) collective-permute-start(bf16[512,1152]{1,0:T(8,128)(2,1)} %get-tuple-element.97.refs_0_.b_emb), channel_id=1, source_target_pairs={{0,192},{1,193},{2,194},{3,195},{4,196},{5,197},{6,198},{7,199},{8... | collective-permute-start | bytes 3538952 | tf_op jit(solution)/shard_map/ppermute | solution.py:300
  12.4 21.8 %conditional.3 = (bf16[512,768]{1,0:T(8,128)(2,1)S(1)}, bf16[512,768]{1,0:T(8,128)(2,1)}, bf16[512,768]{1,0:T(8,128)(2,1)}, bf16[512,768]{1,0:T(8,128)(2,1)}, f32[512,1152]{1,0:T(8,128)}, /*index=5*/f32[512,1152]{1,0:T(8,128)}) conditional(s32[]{:T(128)} %convert_element_type.19, () %tuple.35, (s32[]{:T(128)}, bf16[512,1152]{1,0:T(8,128)(2,1)}, ...), branch_computations={%region_0.0_spmd, %region_1.2_spmd} | conditional | flops 3815386880 | bytes 37820160 | solution.py:344
  12.5 4.0 %convolution_convert_fusion.2 = bf16[512,768]{1,0:T(8,128)(2,1)} fusion(bf16[512,1152]{1,0:T(8,128)(2,1)} %get-tuple-element.34, bf16[512,1152]{1,0:T(8,128)(2,1)} %get-tuple-element.50, pred[]{:T(512)S(6)} %eq.14, s32[]{:T(128)S(6)} %mul.19, s32[768]{0:T(1024)S(1)} %get-tuple-element.121, s32[768]{0:T(1024)S(1)} %get-tuple-element.122, ...), kind=kOutput, calls=%fused_computation.40 | convolution fusion | flops 953843712 | bytes 3159557 | tf_op jit(solution)/shard_map/cond/branch_1_fun/dot_general | solution.py:353
  16.5 2.6 %convolution_convert_fusion = bf16[512,768]{1,0:T(8,128)(2,1)} fusion(bf16[512,1152]{1,0:T(8,128)(2,1)S(1)} %copy-done.5, bf16[512,1152]{1,0:T(8,128)(2,1)S(1)} %copy-done.3, pred[]{:T(512)S(6)} %eq.14, s32[]{:T(128)S(6)} %mul.19, s32[768]{0:T(1024)S(1)} %get-tuple-element.121, s32[768]{0:T(1024)S(1)} %get-tuple-element.122, ...), kind=kOutput, calls=%fused_computation.38 | convolution fusion | flops 953843712 | bytes 3159557 | tf_op jit(solution)/shard_map/cond/branch_1_fun/dot_general | solution.py:353
  19.6 4.0 %convolution_convert_fusion.1 = bf16[512,768]{1,0:T(8,128)(2,1)} fusion(bf16[512,1152]{1,0:T(8,128)(2,1)} %get-tuple-element.50, bf16[512,1152]{1,0:T(8,128)(2,1)} %get-tuple-element.34, pred[]{:T(512)S(6)} %eq.14, s32[]{:T(128)S(6)} %mul.16, s32[768]{0:T(1024)S(1)} %get-tuple-element.121, s32[768]{0:T(1024)S(1)} %get-tuple-element.122, ...), kind=kOutput, calls=%fused_computation.39 | convolution fusion | flops 953843712 | bytes 3159557 | tf_op jit(solution)/shard_map/cond/branch_1_fun/dot_general | solution.py:352
  23.6 1.8 %convolution_convert_fusion.3 = bf16[512,768]{1,0:T(8,128)(2,1)S(1)} fusion(bf16[512,1152]{1,0:T(8,128)(2,1)S(1)} %copy-done.4, bf16[512,1152]{1,0:T(8,128)(2,1)S(1)} %copy-done.6, pred[]{:T(512)S(6)} %eq.14, s32[]{:T(128)S(6)} %mul.16, s32[768]{0:T(1024)S(1)} %get-tuple-element.121, s32[768]{0:T(1024)S(1)} %get-tuple-element.122, ...), kind=kOutput, calls=%fused_computation.41 | convolution fusion | flops 953843712 | bytes 3159557 | tf_op jit(solution)/shard_map/cond/branch_1_fun/dot_general | solution.py:352
  25.4 4.5 %side_first.3 = f32[512,1152]{1,0:T(8,128)} custom-call(bf16[512,1152]{1,0:T(8,128)(2,1)S(1)} %get-tuple-element.52.refs_0_.refs_1_, bf16[512,1152]{1,0:T(8,128)(2,1)} %get-tuple-element.53.refs_1_.refs_0_), custom_call_target="tpu_custom_call" | custom-call | flops 1000 | bytes 1000 | tf_op jit(solution)/shard_map/cond/branch_1_fun/side_first/pallas_call | solution.py:174
  29.9 4.3 %side_first.4 = f32[512,1152]{1,0:T(8,128)} custom-call(bf16[512,1152]{1,0:T(8,128)(2,1)} %get-tuple-element.53.refs_1_.refs_0_, bf16[512,1152]{1,0:T(8,128)(2,1)S(1)} %get-tuple-element.52.refs_0_.refs_1_), custom_call_target="tpu_custom_call" | custom-call | flops 1000 | bytes 1000 | tf_op jit(solution)/shard_map/cond/branch_1_fun/side_first/pallas_call | solution.py:174
  34.2 3.3 %collective-permute-done.5.a_cross = bf16[512,1152]{1,0:T(8,128)(2,1)} collective-permute-done((bf16[512,1152]{1,0:T(8,128)(2,1)S(1)}, bf16[512,1152]{1,0:T(8,128)(2,1)}, u32[]{:S(2)}, u32[]{:S(2)}) %collective-permute-start.5) | collective-permute-done | bytes 1179680 | tf_op jit(solution)/shard_map/ppermute | solution.py:300
  39.5 13.3 %conditional.4 = (bf16[16,336,128]{2,1,0:T(8,128)(2,1)}) conditional(s32[]{:T(128)} %convert_element_type.19, () %tuple.39, (bf16[512,1152]{1,0:T(8,128)(2,1)S(1)}, bf16[512,1152]{1,0:T(8,128)(2,1)}, bf16[512,1152]{1,0:T(8,128)(2,1)}, f32[512,1152]{1,0:T(8,128)}, f32[512,1152]{1,0:T(8,128)}, /*index=5*/f32[512,1]{1,0:T(8,128)}, ...), branch_computations={%region_2.3_spmd, %region_3.4_spmd} | conditional | flops 3000 | bytes 4721640 | solution.py:344
  39.5 7.3 %side_last.2.grad = bf16[1152,512]{1,0:T(8,128)(2,1)S(1)} custom-call(bf16[512,1152]{1,0:T(8,128)(2,1)S(1)} %get-tuple-element.54.refs_0_, bf16[512,1152]{1,0:T(8,128)(2,1)} %get-tuple-element.55.refs_1_, bf16[512,1152]{1,0:T(8,128)(2,1)} %get-tuple-element.56.refs_2_, f32[512,1152]{1,0:T(8,128)} %get-tuple-element.57.refs_3_, ...), custom_call_target="tpu_custom_call" | custom-call | flops 1000 | bytes 1000 | tf_op jit(solution)/shard_map/cond/branch_1_fun/side_last/pallas_call | solution.py:174
  48.0 1.7 %collective-permute-done.grad = bf16[1152,512]{1,0:T(8,128)(2,1)S(1)} collective-permute-done((bf16[1152,512]{1,0:T(8,128)(2,1)S(1)}, bf16[1152,512]{1,0:T(8,128)(2,1)S(1)}, u32[]{:S(2)}, u32[]{:S(2)}) %collective-permute-start) | collective-permute-done | bytes 1179680 | tf_op jit(solution)/shard_map/cond/branch_1_fun/ppermute | solution.py:300
  49.7 3.1 %head_pack.2 = bf16[16,336,128]{2,1,0:T(8,128)(2,1)} custom-call(bf16[1152,512]{1,0:T(8,128)(2,1)S(1)} %collective-permute-done.grad, bf16[512,768]{1,0:T(8,128)(2,1)} %get-tuple-element.60.feats, f32[1152,768]{1,0:T(8,128)S(1)} %head_own.2.before), custom_call_target="tpu_custom_call" | custom-call | flops 1000 | bytes 1000 | tf_op jit(solution)/shard_map/cond/branch_1_fun/head_pack/pallas_call | solution.py:368
  52.8 6.0 %all-to-all-start = ((bf16[4,4,336,128]{3,2,1,0:T(8,128)(2,1)}), bf16[4,4,336,128]{3,2,1,0:T(8,128)(2,1)S(1)}, u32[]{:S(2)}, u32[]{:S(2)}) async-start(bf16[4,4,336,128]{3,2,1,0:T(8,128)(2,1)} %bitcast.3), calls=%async_computation | async-start | bytes 2752512 | tf_op jit(solution)/shard_map/all_to_all | solution.py:381
  58.8 4.5 %side_first.5 = f32[512,1152]{1,0:T(8,128)} custom-call(bf16[512,1152]{1,0:T(8,128)(2,1)} %get-tuple-element.97.refs_0_.b_emb, bf16[512,1152]{1,0:T(8,128)(2,1)S(1)} %collective-permute-done.7.refs_1_.a_from, f32[512,1152]{1,0:T(8,128)} %get-tuple-element.103.refs_2_), custom_call_target="tpu_custom_call" | custom-call | flops 1000 | bytes 1000 | tf_op jit(solution)/shard_map/side_first/pallas_call | solution.py:174
  64.7 10.6 %conditional.5 = (bf16[16,336,128]{2,1,0:T(8,128)(2,1)}) conditional(s32[]{:T(128)} %convert_element_type.19, () %tuple.34, (bf16[512,1152]{1,0:T(8,128)(2,1)}, bf16[512,1152]{1,0:T(8,128)(2,1)}, f32[512,1152]{1,0:T(8,128)}, f32[512,1152]{1,0:T(8,128)}, f32[512,1]{1,0:T(8,128)S(1)}, /*index=5*/bf16[512,768]{1,0:T(8,128)(2,1)}, ...), branch_computations={%region_4.5_spmd, %region_5.6_spmd} | conditional | flops 3000 | bytes 4721640 | solution.py:344
  64.7 4.6 %side_last.3.grad = bf16[1152,512]{1,0:T(8,128)(2,1)S(1)} custom-call(bf16[512,1152]{1,0:T(8,128)(2,1)} %get-tuple-element.62.refs_0_, bf16[512,1152]{1,0:T(8,128)(2,1)} %get-tuple-element.63.refs_1_, f32[512,1152]{1,0:T(8,128)} %get-tuple-element.64.refs_2_, f32[512,1152]{1,0:T(8,128)} %get-tuple-element.65.refs_3_, f32[512,1]{1,0:T(8,128)S(1)} %get-tuple-element.66.refs_4_), custom_call_target="tpu_custom_call" | custom-call | flops 1000 | bytes 1000 | tf_op jit(solution)/shard_map/cond/branch_1_fun/side_last/pallas_call | solution.py:174
  69.4 2.2 %head_own.3.before = f32[1152,768]{1,0:T(8,128)S(1)} custom-call(bf16[1152,512]{1,0:T(8,128)(2,1)S(1)} %side_last.3.grad, bf16[512,768]{1,0:T(8,128)(2,1)} %get-tuple-element.68.feats), custom_call_target="tpu_custom_call" | custom-call | flops 1000 | bytes 1000 | tf_op jit(solution)/shard_map/cond/branch_1_fun/head_own/pallas_call | solution.py:367
  72.2 3.1 %head_pack.3 = bf16[16,336,128]{2,1,0:T(8,128)(2,1)} custom-call(bf16[1152,512]{1,0:T(8,128)(2,1)S(1)} %collective-permute-done.1.grad, bf16[512,768]{1,0:T(8,128)(2,1)} %get-tuple-element.67.feats, f32[1152,768]{1,0:T(8,128)S(1)} %head_own.3.before), custom_call_target="tpu_custom_call" | custom-call | flops 1000 | bytes 1000 | tf_op jit(solution)/shard_map/cond/branch_1_fun/head_pack/pallas_call | solution.py:368
  76.2 8.3 %all-to-all-start.1 = ((bf16[16,336,128]{2,1,0:T(8,128)(2,1)}), bf16[16,336,128]{2,1,0:T(8,128)(2,1)S(1)}, u32[]{:S(2)}, u32[]{:S(2)}) async-start(bf16[16,336,128]{2,1,0:T(8,128)(2,1)} %get-tuple-element.139), calls=%async_computation.1 | async-start | bytes 2752512 | tf_op jit(solution)/shard_map/all_to_all | solution.py:393
  90.1 7.1 %loss.1 = f32[1,512]{1,0:T(1,128)} custom-call(s32[1]{0:T(128)} %bitcast.odd.use_a, bf16[512,1152]{1,0:T(8,128)(2,1)} %copy-done.2, bf16[512,1152]{1,0:T(8,128)(2,1)} %get-tuple-element.97.refs_0_.b_emb, bf16[512,1152]{1,0:T(8,128)(2,1)} %collective-permute-done.5.a_cross, bf16[512,1152]{1,0:T(8,128)(2,1)} %collective-permute-done.6.b_cross, ...), custom_call_target="tpu_custom_call" | custom-call | flops 1000 | bytes 1000 | tf_op jit(solution)/shard_map/loss/pallas_call | solution.py:396
  97.2 8.5 %all-to-all-done.1.b_got = bf16[16,336,128]{2,1,0:T(8,128)(2,1)S(1)} async-done(((bf16[16,336,128]{2,1,0:T(8,128)(2,1)}), bf16[16,336,128]{2,1,0:T(8,128)(2,1)S(1)}, u32[]{:S(2)}, u32[]{:S(2)}) %all-to-all-start.1) | async-done | bytes 1376288 | tf_op jit(solution)/shard_map/all_to_all | solution.py:393
  106.9 21.2 %all_to_all.15.got = f32[8,2,48,128]{3,2,1,0:T(8,128)S(1)} all-to-all(f32[8,2,48,128]{3,2,1,0:T(8,128)S(1)} %add_pack.1), channel_id=1, replica_groups=mesh['y'=4,'xlo'=2,'xhi'=2,'z'=8,'core'=2] {'z'}, dimensions={0} | all-to-all | bytes 786432 | tf_op jit(solution)/shard_map/all_to_all | solution.py:403
  (43 shorter events, 15.7 us)
Async XLA Ops:
  9.6 29.9 %copy-start.2 = (bf16[512,1152]{1,0:T(8,128)(2,1)}, bf16[512,1152]{1,0:T(8,128)(2,1)S(1)}, u32[]{:S(2)}) copy-start(bf16[512,1152]{1,0:T(8,128)(2,1)S(1)} %get-tuple-element.112.a_emb) | copy-start | bytes 3538948
  9.6 27.9 %collective-permute-start.5 = (bf16[512,1152]{1,0:T(8,128)(2,1)S(1)}, bf16[512,1152]{1,0:T(8,128)(2,1)}, u32[]{:S(2)}, u32[]{:S(2)}) collective-permute-start(bf16[512,1152]{1,0:T(8,128)(2,1)S(1)} %get-tuple-element.112.a_emb), channel_id=1, source_target_pairs={{0,32},{1,33},{2,34},{3,35},{4,36},{5,37},{6,38},{7,39},{8,40},{9,... | collective-permute-start | bytes 3538952 | tf_op jit(solution)/shard_map/ppermute | solution.py:300
  10.3 27.7 %collective-permute-start.4 = (bf16[512,1152]{1,0:T(8,128)(2,1)}, bf16[512,1152]{1,0:T(8,128)(2,1)}, u32[]{:S(2)}, u32[]{:S(2)}) collective-permute-start(bf16[512,1152]{1,0:T(8,128)(2,1)} %get-tuple-element.97.refs_0_.b_emb), channel_id=1, source_target_pairs={{0,192},{1,193},{2,194},{3,195},{4,196},{5,197},{6,198},{7,199},{8... | collective-permute-start | bytes 3538952 | tf_op jit(solution)/shard_map/ppermute | solution.py:300
  11.8 27.7 %collective-permute-start.7 = (bf16[512,1152]{1,0:T(8,128)(2,1)S(1)}, bf16[512,1152]{1,0:T(8,128)(2,1)S(1)}, u32[]{:S(2)}, u32[]{:S(2)}) collective-permute-start(bf16[512,1152]{1,0:T(8,128)(2,1)S(1)} %get-tuple-element.112.a_emb), channel_id=1, source_target_pairs={{0,64},{1,65},{2,66},{3,67},{4,68},{5,69},{6,70},{7,71},{8,72},{9,... | collective-permute-start | bytes 3538952 | tf_op jit(solution)/shard_map/ppermute | solution.py:300
  12.5 4.0 %copy-start.3 = (bf16[512,1152]{1,0:T(8,128)(2,1)S(1)}, bf16[512,1152]{1,0:T(8,128)(2,1)}, u32[]{:S(2)}) copy-start(bf16[512,1152]{1,0:T(8,128)(2,1)} %get-tuple-element.34) | copy-start | bytes 3538948 | tf_op jit(solution)/shard_map/cond
  12.5 4.0 %copy-start.5 = (bf16[512,1152]{1,0:T(8,128)(2,1)S(1)}, bf16[512,1152]{1,0:T(8,128)(2,1)}, u32[]{:S(2)}) copy-start(bf16[512,1152]{1,0:T(8,128)(2,1)} %get-tuple-element.50) | copy-start | bytes 3538948 | tf_op jit(solution)/shard_map/cond
  16.5 17.7 %collective-permute-start.2 = (bf16[512,768]{1,0:T(8,128)(2,1)}, bf16[512,768]{1,0:T(8,128)(2,1)}, u32[]{:S(2)}, u32[]{:S(2)}) collective-permute-start(bf16[512,768]{1,0:T(8,128)(2,1)} %convolution_convert_fusion.2), channel_id=1, source_target_pairs={{0,1},{1,0},{2,3},{3,2},{4,5},{5,4},{6,7},{7,6},{8,9},{9,8},{10,11... | collective-permute-start | bytes 2359304 | tf_op jit(solution)/shard_map/cond/branch_1_fun/ppermute | solution.py:300
  19.1 15.2 %collective-permute-start.3 = (bf16[512,768]{1,0:T(8,128)(2,1)}, bf16[512,768]{1,0:T(8,128)(2,1)}, u32[]{:S(2)}, u32[]{:S(2)}) collective-permute-start(bf16[512,768]{1,0:T(8,128)(2,1)} %convolution_convert_fusion), channel_id=1, source_target_pairs={{0,1},{1,0},{2,3},{3,2},{4,5},{5,4},{6,7},{7,6},{8,9},{9,8},{10,11... | collective-permute-start | bytes 2359304 | tf_op jit(solution)/shard_map/cond/branch_1_fun/ppermute | solution.py:300
  19.6 4.0 %copy-start.4 = (bf16[512,1152]{1,0:T(8,128)(2,1)S(1)}, bf16[512,1152]{1,0:T(8,128)(2,1)}, u32[]{:S(2)}) copy-start(bf16[512,1152]{1,0:T(8,128)(2,1)} %get-tuple-element.34) | copy-start | bytes 3538948 | tf_op jit(solution)/shard_map/cond
  19.6 4.0 %copy-start.6 = (bf16[512,1152]{1,0:T(8,128)(2,1)S(1)}, bf16[512,1152]{1,0:T(8,128)(2,1)}, u32[]{:S(2)}) copy-start(bf16[512,1152]{1,0:T(8,128)(2,1)} %get-tuple-element.50) | copy-start | bytes 3538948 | tf_op jit(solution)/shard_map/cond
  38.0 26.7 %collective-permute-start.6 = (bf16[512,1152]{1,0:T(8,128)(2,1)}, bf16[512,1152]{1,0:T(8,128)(2,1)}, u32[]{:S(2)}, u32[]{:S(2)}) collective-permute-start(bf16[512,1152]{1,0:T(8,128)(2,1)} %collective-permute-done.4.b_from), channel_id=1, source_target_pairs={{0,32},{1,33},{2,34},{3,35},{4,36},{5,37},{6,38},{7,39},{8,40},{9,... | collective-permute-start | bytes 3538952 | tf_op jit(solution)/shard_map/ppermute | solution.py:300
  39.5 19.3 %copy-start = (bf16[512,1152]{1,0:T(8,128)(2,1)}, bf16[512,1152]{1,0:T(8,128)(2,1)S(1)}, u32[]{:S(2)}) copy-start(bf16[512,1152]{1,0:T(8,128)(2,1)S(1)} %collective-permute-done.7.refs_1_.a_from) | copy-start | bytes 3538948
  46.8 2.9 %collective-permute-start = (bf16[1152,512]{1,0:T(8,128)(2,1)S(1)}, bf16[1152,512]{1,0:T(8,128)(2,1)S(1)}, u32[]{:S(2)}, u32[]{:S(2)}) collective-permute-start(bf16[1152,512]{1,0:T(8,128)(2,1)S(1)} %side_last.2.grad), channel_id=1, source_target_pairs={{0,1},{1,0},{2,3},{3,2},{4,5},{5,4},{6,7},{7,6},{8,9},{9,8},{10,11... | collective-permute-start | bytes 3538952 | tf_op jit(solution)/shard_map/cond/branch_1_fun/ppermute | solution.py:300
  52.8 23.4 %all-to-all-start = ((bf16[4,4,336,128]{3,2,1,0:T(8,128)(2,1)}), bf16[4,4,336,128]{3,2,1,0:T(8,128)(2,1)S(1)}, u32[]{:S(2)}, u32[]{:S(2)}) async-start(bf16[4,4,336,128]{3,2,1,0:T(8,128)(2,1)} %bitcast.3), calls=%async_computation | async-start | bytes 2752512 | tf_op jit(solution)/shard_map/all_to_all | solution.py:381
  58.8 5.9 %copy-start.7 = (f32[512,1]{1,0:T(8,128)S(1)}, f32[512,1]{1,0:T(8,128)}, u32[]{:S(2)}) copy-start(f32[512,1]{1,0:T(8,128)} %get-tuple-element.111) | copy-start | bytes 6148
  69.3 2.9 %collective-permute-start.1 = (bf16[1152,512]{1,0:T(8,128)(2,1)S(1)}, bf16[1152,512]{1,0:T(8,128)(2,1)S(1)}, u32[]{:S(2)}, u32[]{:S(2)}) collective-permute-start(bf16[1152,512]{1,0:T(8,128)(2,1)S(1)} %side_last.3.grad), channel_id=1, source_target_pairs={{0,1},{1,0},{2,3},{3,2},{4,5},{5,4},{6,7},{7,6},{8,9},{9,8},{10,11... | collective-permute-start | bytes 3538952 | tf_op jit(solution)/shard_map/cond/branch_1_fun/ppermute | solution.py:300
  76.2 29.5 %all-to-all-start.1 = ((bf16[16,336,128]{2,1,0:T(8,128)(2,1)}), bf16[16,336,128]{2,1,0:T(8,128)(2,1)S(1)}, u32[]{:S(2)}, u32[]{:S(2)}) async-start(bf16[16,336,128]{2,1,0:T(8,128)(2,1)} %get-tuple-element.139), calls=%async_computation.1 | async-start | bytes 2752512 | tf_op jit(solution)/shard_map/all_to_all | solution.py:393
  84.7 21.0 %collective-permute-start.10 = (bf16[336,128]{1,0:T(8,128)(2,1)S(1)}, bf16[336,128]{1,0:T(8,128)(2,1)S(1)}, u32[]{:S(2)}, u32[]{:S(2)}) collective-permute-start(bf16[336,128]{1,0:T(8,128)(2,1)S(1)} %get-tuple-element.116), channel_id=1, source_target_pairs={{0,48},{1,49},{2,50},{3,51},{4,52},{5,53},{6,54},{7,55},{8,56},{9,... | collective-permute-start | bytes 258056 | tf_op jit(solution)/shard_map/ppermute | solution.py:300
  86.2 20.1 %collective-permute-start.8 = (bf16[336,128]{1,0:T(8,128)(2,1)S(1)}, bf16[336,128]{1,0:T(8,128)(2,1)S(1)}, u32[]{:S(2)}, u32[]{:S(2)}) collective-permute-start(bf16[336,128]{1,0:T(8,128)(2,1)S(1)} %get-tuple-element.114), channel_id=1, source_target_pairs={{0,16},{1,17},{2,18},{3,19},{4,20},{5,21},{6,22},{7,23},{8,24},{9,... | collective-permute-start | bytes 258056 | tf_op jit(solution)/shard_map/ppermute | solution.py:300
  87.4 18.9 %collective-permute-start.9 = (bf16[336,128]{1,0:T(8,128)(2,1)S(1)}, bf16[336,128]{1,0:T(8,128)(2,1)S(1)}, u32[]{:S(2)}, u32[]{:S(2)}) collective-permute-start(bf16[336,128]{1,0:T(8,128)(2,1)S(1)} %get-tuple-element.115), channel_id=1, source_target_pairs={{0,32},{1,33},{2,34},{3,35},{4,36},{5,37},{6,38},{7,39},{8,40},{9,... | collective-permute-start | bytes 258056 | tf_op jit(solution)/shard_map/ppermute | solution.py:300
  88.9 1.3 copy-start.1

commit v4 on v3

--- a/solution.py
+++ b/solution.py
@@ -126,7 +126,7 @@
     bufs = take(len(sources))
     held = None if last else take(1)[0]
     in_sems, out_sems = refs
-    block = 256
+    block = 512
     parts = [pl.ds(i * block, block) for i in range(ROWS // block)]
     loads = {}
     for k in range(1 + count):

time: 130 us -> 130 us (level)
  transfers between devices with their start and end apart: 13 -> 13, of which waited for: 8 -> 8; matrix products, arithmetic and copies ran while one was open for 10% -> 10% of each run, Pallas kernels for 32% -> 33%
where the time goes in v4:
time: 130 us; the launch traced here: 129 us
  Pallas kernels  53 us (41%)
  starting transfers between devices  23.5 us (18%)
  blocking collectives  21.2 us (16%)
  waiting for transfers between devices  16.7 us (13%)
  matrix products  12.4 us (10%)
  local copies, waits for them, and re-layouts  1.3 us (1%)
    pallas_call x5, Pallas kernels, side(): call(functools.partial(side_kernel, len(partners), diagonal, adds, last),...  25.9 us
    all_to_all x1, blocking collectives, body(): got = lax.all_to_all(part, 'z', 0, 0)  21.2 us
    ppermute x11, starting transfers between devices, move(): return lax.ppermute(value, AXES, pairs)  9.16 us
    pallas_call x1, Pallas kernels, embed(): call(embed_kernel, 'embed', [SMEM(), HBM(), HBM(), HBM(), HBM()], one + o...  8.99 us
    all_to_all x1, waiting for transfers between devices, body(): b_got = lax.all_to_all(b_terms, ('y', 'xlo', 'xhi'), 0, 0)  8.47 us
    all_to_all x1, starting transfers between devices, body(): b_got = lax.all_to_all(b_terms, ('y', 'xlo', 'xhi'), 0, 0)  8.35 us
    ppermute x11, waiting for transfers between devices, move(): return lax.ppermute(value, AXES, pairs)  7.39 us
    pallas_call x1, Pallas kernels, body(): call(loss_kernel, 'loss', [SMEM()] + [VMEM()] * 6, shape((1, ROWS), F32))  7.1 us
  transfers between devices with their start and end apart: 13, of which 8 were waited for; matrix products, arithmetic and copies ran while one was open for 10% of the time, Pallas kernels for 33%

profile of v4, /device:TPU:10, one launch (start us, length us, event | category | flops | bytes accessed | tf_op | source)
XLA Modules:
  0.0 129.0 jit_solution(15564478221421948062)
XLA Ops:
  0.6 9.0 %embed.1 = (bf16[512,1152]{1,0:T(8,128)(2,1)S(1)}, f32[512,1152]{1,0:T(8,128)}, f32[512,1]{1,0:T(8,128)}, bf16[512,1152]{1,0:T(8,128)(2,1)}, f32[512,1152]{1,0:T(8,128)}, /*index=5*/f32[512,1]{1,0:T(8,128)}) custom-call(s32[1]{0:T(128)} %bitcast.odd.use_a, bf16[512,1152]{1,0:T(8,128)(2,1)} %image_feats.1, bf16[512,1152]{1,0:T(8,128)(2,1)} %text_feats.1, ...), custom_call_target="tpu_custom_call" | custom-call | flops 1000 | bytes 1000 | tf_op jit(solution)/shard_map/embed/pallas_call | solution.py:90
  10.3 1.6 %collective-permute-start.4 = (bf16[512,1152]{1,0:T(8,128)(2,1)}, bf16[512,1152]{1,0:T(8,128)(2,1)}, u32[]{:S(2)}, u32[]{:S(2)}) collective-permute-start(bf16[512,1152]{1,0:T(8,128)(2,1)} %get-tuple-element.97.refs_0_.b_emb), channel_id=1, source_target_pairs={{0,192},{1,193},{2,194},{3,195},{4,196},{5,197},{6,198},{7,199},{8... | collective-permute-start | bytes 3538952 | tf_op jit(solution)/shard_map/ppermute | solution.py:300
  12.4 22.2 %conditional.3 = (bf16[512,768]{1,0:T(8,128)(2,1)S(1)}, bf16[512,768]{1,0:T(8,128)(2,1)}, bf16[512,768]{1,0:T(8,128)(2,1)}, bf16[512,768]{1,0:T(8,128)(2,1)}, f32[512,1152]{1,0:T(8,128)}, /*index=5*/f32[512,1152]{1,0:T(8,128)}) conditional(s32[]{:T(128)} %convert_element_type.19, () %tuple.35, (s32[]{:T(128)}, bf16[512,1152]{1,0:T(8,128)(2,1)}, ...), branch_computations={%region_0.0_spmd, %region_1.2_spmd} | conditional | flops 3815386880 | bytes 37820160 | solution.py:344
  12.5 4.0 %convolution_convert_fusion.2 = bf16[512,768]{1,0:T(8,128)(2,1)} fusion(bf16[512,1152]{1,0:T(8,128)(2,1)} %get-tuple-element.34, bf16[512,1152]{1,0:T(8,128)(2,1)} %get-tuple-element.50, pred[]{:T(512)S(6)} %eq.14, s32[]{:T(128)S(6)} %mul.19, s32[768]{0:T(1024)S(1)} %get-tuple-element.121, s32[768]{0:T(1024)S(1)} %get-tuple-element.122, ...), kind=kOutput, calls=%fused_computation.40 | convolution fusion | flops 953843712 | bytes 3159557 | tf_op jit(solution)/shard_map/cond/branch_1_fun/dot_general | solution.py:353
  16.5 2.6 %convolution_convert_fusion = bf16[512,768]{1,0:T(8,128)(2,1)} fusion(bf16[512,1152]{1,0:T(8,128)(2,1)S(1)} %copy-done.5, bf16[512,1152]{1,0:T(8,128)(2,1)S(1)} %copy-done.3, pred[]{:T(512)S(6)} %eq.14, s32[]{:T(128)S(6)} %mul.19, s32[768]{0:T(1024)S(1)} %get-tuple-element.121, s32[768]{0:T(1024)S(1)} %get-tuple-element.122, ...), kind=kOutput, calls=%fused_computation.38 | convolution fusion | flops 953843712 | bytes 3159557 | tf_op jit(solution)/shard_map/cond/branch_1_fun/dot_general | solution.py:353
  19.6 4.0 %convolution_convert_fusion.1 = bf16[512,768]{1,0:T(8,128)(2,1)} fusion(bf16[512,1152]{1,0:T(8,128)(2,1)} %get-tuple-element.50, bf16[512,1152]{1,0:T(8,128)(2,1)} %get-tuple-element.34, pred[]{:T(512)S(6)} %eq.14, s32[]{:T(128)S(6)} %mul.16, s32[768]{0:T(1024)S(1)} %get-tuple-element.121, s32[768]{0:T(1024)S(1)} %get-tuple-element.122, ...), kind=kOutput, calls=%fused_computation.39 | convolution fusion | flops 953843712 | bytes 3159557 | tf_op jit(solution)/shard_map/cond/branch_1_fun/dot_general | solution.py:352
  23.6 1.8 %convolution_convert_fusion.3 = bf16[512,768]{1,0:T(8,128)(2,1)S(1)} fusion(bf16[512,1152]{1,0:T(8,128)(2,1)S(1)} %copy-done.4, bf16[512,1152]{1,0:T(8,128)(2,1)S(1)} %copy-done.6, pred[]{:T(512)S(6)} %eq.14, s32[]{:T(128)S(6)} %mul.16, s32[768]{0:T(1024)S(1)} %get-tuple-element.121, s32[768]{0:T(1024)S(1)} %get-tuple-element.122, ...), kind=kOutput, calls=%fused_computation.41 | convolution fusion | flops 953843712 | bytes 3159557 | tf_op jit(solution)/shard_map/cond/branch_1_fun/dot_general | solution.py:352
  25.4 4.7 %side_first.3 = f32[512,1152]{1,0:T(8,128)} custom-call(bf16[512,1152]{1,0:T(8,128)(2,1)S(1)} %get-tuple-element.52.refs_0_.refs_1_, bf16[512,1152]{1,0:T(8,128)(2,1)} %get-tuple-element.53.refs_1_.refs_0_), custom_call_target="tpu_custom_call" | custom-call | flops 1000 | bytes 1000 | tf_op jit(solution)/shard_map/cond/branch_1_fun/side_first/pallas_call | solution.py:174
  30.1 4.5 %side_first.4 = f32[512,1152]{1,0:T(8,128)} custom-call(bf16[512,1152]{1,0:T(8,128)(2,1)} %get-tuple-element.53.refs_1_.refs_0_, bf16[512,1152]{1,0:T(8,128)(2,1)S(1)} %get-tuple-element.52.refs_0_.refs_1_), custom_call_target="tpu_custom_call" | custom-call | flops 1000 | bytes 1000 | tf_op jit(solution)/shard_map/cond/branch_1_fun/side_first/pallas_call | solution.py:174
  34.7 2.8 %collective-permute-done.5.a_cross = bf16[512,1152]{1,0:T(8,128)(2,1)} collective-permute-done((bf16[512,1152]{1,0:T(8,128)(2,1)S(1)}, bf16[512,1152]{1,0:T(8,128)(2,1)}, u32[]{:S(2)}, u32[]{:S(2)}) %collective-permute-start.5) | collective-permute-done | bytes 1179680 | tf_op jit(solution)/shard_map/ppermute | solution.py:300
  39.5 13.2 %conditional.4 = (bf16[16,336,128]{2,1,0:T(8,128)(2,1)}) conditional(s32[]{:T(128)} %convert_element_type.19, () %tuple.39, (bf16[512,1152]{1,0:T(8,128)(2,1)S(1)}, bf16[512,1152]{1,0:T(8,128)(2,1)}, bf16[512,1152]{1,0:T(8,128)(2,1)}, f32[512,1152]{1,0:T(8,128)}, f32[512,1152]{1,0:T(8,128)}, /*index=5*/f32[512,1]{1,0:T(8,128)}, ...), branch_computations={%region_2.3_spmd, %region_3.4_spmd} | conditional | flops 3000 | bytes 4721640 | solution.py:344
  39.5 7.2 %side_last.2.grad = bf16[1152,512]{1,0:T(8,128)(2,1)S(1)} custom-call(bf16[512,1152]{1,0:T(8,128)(2,1)S(1)} %get-tuple-element.54.refs_0_, bf16[512,1152]{1,0:T(8,128)(2,1)} %get-tuple-element.55.refs_1_, bf16[512,1152]{1,0:T(8,128)(2,1)} %get-tuple-element.56.refs_2_, f32[512,1152]{1,0:T(8,128)} %get-tuple-element.57.refs_3_, ...), custom_call_target="tpu_custom_call" | custom-call | flops 1000 | bytes 1000 | tf_op jit(solution)/shard_map/cond/branch_1_fun/side_last/pallas_call | solution.py:174
  47.9 1.7 %collective-permute-done.grad = bf16[1152,512]{1,0:T(8,128)(2,1)S(1)} collective-permute-done((bf16[1152,512]{1,0:T(8,128)(2,1)S(1)}, bf16[1152,512]{1,0:T(8,128)(2,1)S(1)}, u32[]{:S(2)}, u32[]{:S(2)}) %collective-permute-start) | collective-permute-done | bytes 1179680 | tf_op jit(solution)/shard_map/cond/branch_1_fun/ppermute | solution.py:300
  49.7 3.1 %head_pack.2 = bf16[16,336,128]{2,1,0:T(8,128)(2,1)} custom-call(bf16[1152,512]{1,0:T(8,128)(2,1)S(1)} %collective-permute-done.grad, bf16[512,768]{1,0:T(8,128)(2,1)} %get-tuple-element.60.feats, f32[1152,768]{1,0:T(8,128)S(1)} %head_own.2.before), custom_call_target="tpu_custom_call" | custom-call | flops 1000 | bytes 1000 | tf_op jit(solution)/shard_map/cond/branch_1_fun/head_pack/pallas_call | solution.py:368
  52.8 6.0 %all-to-all-start = ((bf16[4,4,336,128]{3,2,1,0:T(8,128)(2,1)}), bf16[4,4,336,128]{3,2,1,0:T(8,128)(2,1)S(1)}, u32[]{:S(2)}, u32[]{:S(2)}) async-start(bf16[4,4,336,128]{3,2,1,0:T(8,128)(2,1)} %bitcast.3), calls=%async_computation | async-start | bytes 2752512 | tf_op jit(solution)/shard_map/all_to_all | solution.py:381
  58.7 4.8 %side_first.5 = f32[512,1152]{1,0:T(8,128)} custom-call(bf16[512,1152]{1,0:T(8,128)(2,1)} %get-tuple-element.97.refs_0_.b_emb, bf16[512,1152]{1,0:T(8,128)(2,1)S(1)} %collective-permute-done.7.refs_1_.a_from, f32[512,1152]{1,0:T(8,128)} %get-tuple-element.103.refs_2_), custom_call_target="tpu_custom_call" | custom-call | flops 1000 | bytes 1000 | tf_op jit(solution)/shard_map/side_first/pallas_call | solution.py:174
  64.7 10.6 %conditional.5 = (bf16[16,336,128]{2,1,0:T(8,128)(2,1)}) conditional(s32[]{:T(128)} %convert_element_type.19, () %tuple.34, (bf16[512,1152]{1,0:T(8,128)(2,1)}, bf16[512,1152]{1,0:T(8,128)(2,1)}, f32[512,1152]{1,0:T(8,128)}, f32[512,1152]{1,0:T(8,128)}, f32[512,1]{1,0:T(8,128)S(1)}, /*index=5*/bf16[512,768]{1,0:T(8,128)(2,1)}, ...), branch_computations={%region_4.5_spmd, %region_5.6_spmd} | conditional | flops 3000 | bytes 4721640 | solution.py:344
  64.7 4.6 %side_last.3.grad = bf16[1152,512]{1,0:T(8,128)(2,1)S(1)} custom-call(bf16[512,1152]{1,0:T(8,128)(2,1)} %get-tuple-element.62.refs_0_, bf16[512,1152]{1,0:T(8,128)(2,1)} %get-tuple-element.63.refs_1_, f32[512,1152]{1,0:T(8,128)} %get-tuple-element.64.refs_2_, f32[512,1152]{1,0:T(8,128)} %get-tuple-element.65.refs_3_, f32[512,1]{1,0:T(8,128)S(1)} %get-tuple-element.66.refs_4_), custom_call_target="tpu_custom_call" | custom-call | flops 1000 | bytes 1000 | tf_op jit(solution)/shard_map/cond/branch_1_fun/side_last/pallas_call | solution.py:174
  69.4 2.2 %head_own.3.before = f32[1152,768]{1,0:T(8,128)S(1)} custom-call(bf16[1152,512]{1,0:T(8,128)(2,1)S(1)} %side_last.3.grad, bf16[512,768]{1,0:T(8,128)(2,1)} %get-tuple-element.68.feats), custom_call_target="tpu_custom_call" | custom-call | flops 1000 | bytes 1000 | tf_op jit(solution)/shard_map/cond/branch_1_fun/head_own/pallas_call | solution.py:367
  72.2 3.1 %head_pack.3 = bf16[16,336,128]{2,1,0:T(8,128)(2,1)} custom-call(bf16[1152,512]{1,0:T(8,128)(2,1)S(1)} %collective-permute-done.1.grad, bf16[512,768]{1,0:T(8,128)(2,1)} %get-tuple-element.67.feats, f32[1152,768]{1,0:T(8,128)S(1)} %head_own.3.before), custom_call_target="tpu_custom_call" | custom-call | flops 1000 | bytes 1000 | tf_op jit(solution)/shard_map/cond/branch_1_fun/head_pack/pallas_call | solution.py:368
  76.2 8.3 %all-to-all-start.1 = ((bf16[16,336,128]{2,1,0:T(8,128)(2,1)}), bf16[16,336,128]{2,1,0:T(8,128)(2,1)S(1)}, u32[]{:S(2)}, u32[]{:S(2)}) async-start(bf16[16,336,128]{2,1,0:T(8,128)(2,1)} %get-tuple-element.139), calls=%async_computation.1 | async-start | bytes 2752512 | tf_op jit(solution)/shard_map/all_to_all | solution.py:393
  90.1 7.1 %loss.1 = f32[1,512]{1,0:T(1,128)} custom-call(s32[1]{0:T(128)} %bitcast.odd.use_a, bf16[512,1152]{1,0:T(8,128)(2,1)} %copy-done.2, bf16[512,1152]{1,0:T(8,128)(2,1)} %get-tuple-element.97.refs_0_.b_emb, bf16[512,1152]{1,0:T(8,128)(2,1)} %collective-permute-done.5.a_cross, bf16[512,1152]{1,0:T(8,128)(2,1)} %collective-permute-done.6.b_cross, ...), custom_call_target="tpu_custom_call" | custom-call | flops 1000 | bytes 1000 | tf_op jit(solution)/shard_map/loss/pallas_call | solution.py:396
  97.2 8.5 %all-to-all-done.1.b_got = bf16[16,336,128]{2,1,0:T(8,128)(2,1)S(1)} async-done(((bf16[16,336,128]{2,1,0:T(8,128)(2,1)}), bf16[16,336,128]{2,1,0:T(8,128)(2,1)S(1)}, u32[]{:S(2)}, u32[]{:S(2)}) %all-to-all-start.1) | async-done | bytes 1376288 | tf_op jit(solution)/shard_map/all_to_all | solution.py:393
  106.9 21.2 %all_to_all.15.got = f32[8,2,48,128]{3,2,1,0:T(8,128)S(1)} all-to-all(f32[8,2,48,128]{3,2,1,0:T(8,128)S(1)} %add_pack.1), channel_id=1, replica_groups=mesh['y'=4,'xlo'=2,'xhi'=2,'z'=8,'core'=2] {'z'}, dimensions={0} | all-to-all | bytes 786432 | tf_op jit(solution)/shard_map/all_to_all | solution.py:403
  (43 shorter events, 15.3 us)
Async XLA Ops:
  9.6 29.9 %copy-start.2 = (bf16[512,1152]{1,0:T(8,128)(2,1)}, bf16[512,1152]{1,0:T(8,128)(2,1)S(1)}, u32[]{:S(2)}) copy-start(bf16[512,1152]{1,0:T(8,128)(2,1)S(1)} %get-tuple-element.112.a_emb) | copy-start | bytes 3538948
  9.6 27.9 %collective-permute-start.5 = (bf16[512,1152]{1,0:T(8,128)(2,1)S(1)}, bf16[512,1152]{1,0:T(8,128)(2,1)}, u32[]{:S(2)}, u32[]{:S(2)}) collective-permute-start(bf16[512,1152]{1,0:T(8,128)(2,1)S(1)} %get-tuple-element.112.a_emb), channel_id=1, source_target_pairs={{0,32},{1,33},{2,34},{3,35},{4,36},{5,37},{6,38},{7,39},{8,40},{9,... | collective-permute-start | bytes 3538952 | tf_op jit(solution)/shard_map/ppermute | solution.py:300
  10.3 27.7 %collective-permute-start.4 = (bf16[512,1152]{1,0:T(8,128)(2,1)}, bf16[512,1152]{1,0:T(8,128)(2,1)}, u32[]{:S(2)}, u32[]{:S(2)}) collective-permute-start(bf16[512,1152]{1,0:T(8,128)(2,1)} %get-tuple-element.97.refs_0_.b_emb), channel_id=1, source_target_pairs={{0,192},{1,193},{2,194},{3,195},{4,196},{5,197},{6,198},{7,199},{8... | collective-permute-start | bytes 3538952 | tf_op jit(solution)/shard_map/ppermute | solution.py:300
  11.8 27.7 %collective-permute-start.7 = (bf16[512,1152]{1,0:T(8,128)(2,1)S(1)}, bf16[512,1152]{1,0:T(8,128)(2,1)S(1)}, u32[]{:S(2)}, u32[]{:S(2)}) collective-permute-start(bf16[512,1152]{1,0:T(8,128)(2,1)S(1)} %get-tuple-element.112.a_emb), channel_id=1, source_target_pairs={{0,64},{1,65},{2,66},{3,67},{4,68},{5,69},{6,70},{7,71},{8,72},{9,... | collective-permute-start | bytes 3538952 | tf_op jit(solution)/shard_map/ppermute | solution.py:300
  12.5 4.0 %copy-start.3 = (bf16[512,1152]{1,0:T(8,128)(2,1)S(1)}, bf16[512,1152]{1,0:T(8,128)(2,1)}, u32[]{:S(2)}) copy-start(bf16[512,1152]{1,0:T(8,128)(2,1)} %get-tuple-element.34) | copy-start | bytes 3538948 | tf_op jit(solution)/shard_map/cond
  12.5 4.0 %copy-start.5 = (bf16[512,1152]{1,0:T(8,128)(2,1)S(1)}, bf16[512,1152]{1,0:T(8,128)(2,1)}, u32[]{:S(2)}) copy-start(bf16[512,1152]{1,0:T(8,128)(2,1)} %get-tuple-element.50) | copy-start | bytes 3538948 | tf_op jit(solution)/shard_map/cond
  16.5 18.2 %collective-permute-start.2 = (bf16[512,768]{1,0:T(8,128)(2,1)}, bf16[512,768]{1,0:T(8,128)(2,1)}, u32[]{:S(2)}, u32[]{:S(2)}) collective-permute-start(bf16[512,768]{1,0:T(8,128)(2,1)} %convolution_convert_fusion.2), channel_id=1, source_target_pairs={{0,1},{1,0},{2,3},{3,2},{4,5},{5,4},{6,7},{7,6},{8,9},{9,8},{10,11... | collective-permute-start | bytes 2359304 | tf_op jit(solution)/shard_map/cond/branch_1_fun/ppermute | solution.py:300
  19.1 15.6 %collective-permute-start.3 = (bf16[512,768]{1,0:T(8,128)(2,1)}, bf16[512,768]{1,0:T(8,128)(2,1)}, u32[]{:S(2)}, u32[]{:S(2)}) collective-permute-start(bf16[512,768]{1,0:T(8,128)(2,1)} %convolution_convert_fusion), channel_id=1, source_target_pairs={{0,1},{1,0},{2,3},{3,2},{4,5},{5,4},{6,7},{7,6},{8,9},{9,8},{10,11... | collective-permute-start | bytes 2359304 | tf_op jit(solution)/shard_map/cond/branch_1_fun/ppermute | solution.py:300
  19.6 4.0 %copy-start.4 = (bf16[512,1152]{1,0:T(8,128)(2,1)S(1)}, bf16[512,1152]{1,0:T(8,128)(2,1)}, u32[]{:S(2)}) copy-start(bf16[512,1152]{1,0:T(8,128)(2,1)} %get-tuple-element.34) | copy-start | bytes 3538948 | tf_op jit(solution)/shard_map/cond
  19.6 4.0 %copy-start.6 = (bf16[512,1152]{1,0:T(8,128)(2,1)S(1)}, bf16[512,1152]{1,0:T(8,128)(2,1)}, u32[]{:S(2)}) copy-start(bf16[512,1152]{1,0:T(8,128)(2,1)} %get-tuple-element.50) | copy-start | bytes 3538948 | tf_op jit(solution)/shard_map/cond
  38.0 26.7 %collective-permute-start.6 = (bf16[512,1152]{1,0:T(8,128)(2,1)}, bf16[512,1152]{1,0:T(8,128)(2,1)}, u32[]{:S(2)}, u32[]{:S(2)}) collective-permute-start(bf16[512,1152]{1,0:T(8,128)(2,1)} %collective-permute-done.4.b_from), channel_id=1, source_target_pairs={{0,32},{1,33},{2,34},{3,35},{4,36},{5,37},{6,38},{7,39},{8,40},{9,... | collective-permute-start | bytes 3538952 | tf_op jit(solution)/shard_map/ppermute | solution.py:300
  39.5 19.2 %copy-start = (bf16[512,1152]{1,0:T(8,128)(2,1)}, bf16[512,1152]{1,0:T(8,128)(2,1)S(1)}, u32[]{:S(2)}) copy-start(bf16[512,1152]{1,0:T(8,128)(2,1)S(1)} %collective-permute-done.7.refs_1_.a_from) | copy-start | bytes 3538948
  46.7 2.9 %collective-permute-start = (bf16[1152,512]{1,0:T(8,128)(2,1)S(1)}, bf16[1152,512]{1,0:T(8,128)(2,1)S(1)}, u32[]{:S(2)}, u32[]{:S(2)}) collective-permute-start(bf16[1152,512]{1,0:T(8,128)(2,1)S(1)} %side_last.2.grad), channel_id=1, source_target_pairs={{0,1},{1,0},{2,3},{3,2},{4,5},{5,4},{6,7},{7,6},{8,9},{9,8},{10,11... | collective-permute-start | bytes 3538952 | tf_op jit(solution)/shard_map/cond/branch_1_fun/ppermute | solution.py:300
  52.8 23.4 %all-to-all-start = ((bf16[4,4,336,128]{3,2,1,0:T(8,128)(2,1)}), bf16[4,4,336,128]{3,2,1,0:T(8,128)(2,1)S(1)}, u32[]{:S(2)}, u32[]{:S(2)}) async-start(bf16[4,4,336,128]{3,2,1,0:T(8,128)(2,1)} %bitcast.3), calls=%async_computation | async-start | bytes 2752512 | tf_op jit(solution)/shard_map/all_to_all | solution.py:381
  58.7 6.0 %copy-start.7 = (f32[512,1]{1,0:T(8,128)S(1)}, f32[512,1]{1,0:T(8,128)}, u32[]{:S(2)}) copy-start(f32[512,1]{1,0:T(8,128)} %get-tuple-element.111) | copy-start | bytes 6148
  69.3 2.9 %collective-permute-start.1 = (bf16[1152,512]{1,0:T(8,128)(2,1)S(1)}, bf16[1152,512]{1,0:T(8,128)(2,1)S(1)}, u32[]{:S(2)}, u32[]{:S(2)}) collective-permute-start(bf16[1152,512]{1,0:T(8,128)(2,1)S(1)} %side_last.3.grad), channel_id=1, source_target_pairs={{0,1},{1,0},{2,3},{3,2},{4,5},{5,4},{6,7},{7,6},{8,9},{9,8},{10,11... | collective-permute-start | bytes 3538952 | tf_op jit(solution)/shard_map/cond/branch_1_fun/ppermute | solution.py:300
  76.2 29.5 %all-to-all-start.1 = ((bf16[16,336,128]{2,1,0:T(8,128)(2,1)}), bf16[16,336,128]{2,1,0:T(8,128)(2,1)S(1)}, u32[]{:S(2)}, u32[]{:S(2)}) async-start(bf16[16,336,128]{2,1,0:T(8,128)(2,1)} %get-tuple-element.139), calls=%async_computation.1 | async-start | bytes 2752512 | tf_op jit(solution)/shard_map/all_to_all | solution.py:393
  84.7 21.0 %collective-permute-start.10 = (bf16[336,128]{1,0:T(8,128)(2,1)S(1)}, bf16[336,128]{1,0:T(8,128)(2,1)S(1)}, u32[]{:S(2)}, u32[]{:S(2)}) collective-permute-start(bf16[336,128]{1,0:T(8,128)(2,1)S(1)} %get-tuple-element.116), channel_id=1, source_target_pairs={{0,48},{1,49},{2,50},{3,51},{4,52},{5,53},{6,54},{7,55},{8,56},{9,... | collective-permute-start | bytes 258056 | tf_op jit(solution)/shard_map/ppermute | solution.py:300
  86.2 20.1 %collective-permute-start.8 = (bf16[336,128]{1,0:T(8,128)(2,1)S(1)}, bf16[336,128]{1,0:T(8,128)(2,1)S(1)}, u32[]{:S(2)}, u32[]{:S(2)}) collective-permute-start(bf16[336,128]{1,0:T(8,128)(2,1)S(1)} %get-tuple-element.114), channel_id=1, source_target_pairs={{0,16},{1,17},{2,18},{3,19},{4,20},{5,21},{6,22},{7,23},{8,24},{9,... | collective-permute-start | bytes 258056 | tf_op jit(solution)/shard_map/ppermute | solution.py:300
  87.4 18.9 %collective-permute-start.9 = (bf16[336,128]{1,0:T(8,128)(2,1)S(1)}, bf16[336,128]{1,0:T(8,128)(2,1)S(1)}, u32[]{:S(2)}, u32[]{:S(2)}) collective-permute-start(bf16[336,128]{1,0:T(8,128)(2,1)S(1)} %get-tuple-element.115), channel_id=1, source_target_pairs={{0,32},{1,33},{2,34},{3,35},{4,36},{5,37},{6,38},{7,39},{8,40},{9,... | collective-permute-start | bytes 258056 | tf_op jit(solution)/shard_map/ppermute | solution.py:300
  88.9 1.3 copy-start.1

commit v5 on v3

--- a/solution.py
+++ b/solution.py
@@ -268,14 +268,14 @@
                 total = total + b_got[4 * y + 2 * (1 - head) + xhi].astype(F32)
 
         def store(z, value, head=head):
-            out[z, head] = value
+            out[z, head] = value.astype(BF16)
 
         repack(total, store)
 
 
 def finish_kernel(got, text, image):
     for head, out in enumerate((text, image)):
-        turned = jnp.sum(got[:, head], axis=0).T
+        turned = jnp.sum(got[:, head].astype(F32), axis=0).T
         parts = []
         for g in range(3):
             parts.append(jnp.concatenate([turned[32 * g : 32 * g + 32], turned[96 + 4 * g : 100 + 4 * g]], axis=0))
@@ -397,7 +397,7 @@
         flag, loss_emb, b_emb, a_cross, b_cross, a_from, b_from
     )
     (b_got,) = after((b_got,), row_loss)
-    part = call(add_pack_kernel, "add_pack", [SMEM()] + [VMEM()] * 5, shape((8, 2, 48, 128), F32))(
+    part = call(add_pack_kernel, "add_pack", [SMEM()] + [VMEM()] * 5, shape((8, 2, 48, 128), BF16))(
         flag, keep, near, cross, corner, b_got
     )
     got = lax.all_to_all(part, "z", 0, 0)

time: 130 us -> 126 us (0.969)
  blocking collectives: 21.2 us -> 18.1 us
    all_to_all x1, blocking collectives: 21.2 us -> 18.1 us  [body(): got = lax.all_to_all(part, 'z', 0, 0)]
  transfers between devices with their start and end apart: 13 -> 13, of which waited for: 8 -> 8; matrix products, arithmetic and copies ran while one was open for 10% -> 10% of each run, Pallas kernels for 32% -> 33%
where the time goes in v5:
time: 126 us
  Pallas kernels  52.1 us (41%)
  starting transfers between devices  23.4 us (19%)
  blocking collectives  18.1 us (14%)
  waiting for transfers between devices  17.6 us (14%)
  matrix products  12.4 us (10%)
  local copies, waits for them, and re-layouts  1.3 us (1%)
    pallas_call x5, Pallas kernels, side(): call(functools.partial(side_kernel, len(partners), diagonal, adds, last),...  25.1 us
    all_to_all x1, blocking collectives, body(): got = lax.all_to_all(part, 'z', 0, 0)  18.1 us
    ppermute x11, starting transfers between devices, move(): return lax.ppermute(value, AXES, pairs)  9.16 us
    pallas_call x1, Pallas kernels, embed(): call(embed_kernel, 'embed', [SMEM(), HBM(), HBM(), HBM(), HBM()], one + o...  8.99 us
    all_to_all x1, waiting for transfers between devices, body(): b_got = lax.all_to_all(b_terms, ('y', 'xlo', 'xhi'), 0, 0)  8.47 us
    all_to_all x1, starting transfers between devices, body(): b_got = lax.all_to_all(b_terms, ('y', 'xlo', 'xhi'), 0, 0)  8.3 us
    ppermute x11, waiting for transfers between devices, move(): return lax.ppermute(value, AXES, pairs)  8.2 us
    pallas_call x1, Pallas kernels, body(): call(loss_kernel, 'loss', [SMEM()] + [VMEM()] * 6, shape((1, ROWS), F32))  7.1 us
  transfers between devices with their start and end apart: 13, of which 8 were waited for; matrix products, arithmetic and copies ran while one was open for 10% of the time, Pallas kernels for 33%

profile of v5, /device:TPU:10, one launch (start us, length us, event | category | flops | bytes accessed | tf_op | source)
XLA Modules:
  0.0 125.6 jit_solution(7293028909283216898)
XLA Ops:
  0.6 9.0 %embed.1 = (bf16[512,1152]{1,0:T(8,128)(2,1)S(1)}, f32[512,1152]{1,0:T(8,128)}, f32[512,1]{1,0:T(8,128)}, bf16[512,1152]{1,0:T(8,128)(2,1)}, f32[512,1152]{1,0:T(8,128)}, /*index=5*/f32[512,1]{1,0:T(8,128)}) custom-call(s32[1]{0:T(128)} %bitcast.odd.use_a, bf16[512,1152]{1,0:T(8,128)(2,1)} %image_feats.1, bf16[512,1152]{1,0:T(8,128)(2,1)} %text_feats.1, ...), custom_call_target="tpu_custom_call" | custom-call | flops 1000 | bytes 1000 | tf_op jit(solution)/shard_map/embed/pallas_call | solution.py:90
  10.3 1.6 %collective-permute-start.4 = (bf16[512,1152]{1,0:T(8,128)(2,1)}, bf16[512,1152]{1,0:T(8,128)(2,1)}, u32[]{:S(2)}, u32[]{:S(2)}) collective-permute-start(bf16[512,1152]{1,0:T(8,128)(2,1)} %get-tuple-element.97.refs_0_.b_emb), channel_id=1, source_target_pairs={{0,192},{1,193},{2,194},{3,195},{4,196},{5,197},{6,198},{7,199},{8... | collective-permute-start | bytes 3538952 | tf_op jit(solution)/shard_map/ppermute | solution.py:300
  12.4 21.8 %conditional.3 = (bf16[512,768]{1,0:T(8,128)(2,1)S(1)}, bf16[512,768]{1,0:T(8,128)(2,1)}, bf16[512,768]{1,0:T(8,128)(2,1)}, bf16[512,768]{1,0:T(8,128)(2,1)}, f32[512,1152]{1,0:T(8,128)}, /*index=5*/f32[512,1152]{1,0:T(8,128)}) conditional(s32[]{:T(128)} %convert_element_type.19, () %tuple.35, (s32[]{:T(128)}, bf16[512,1152]{1,0:T(8,128)(2,1)}, ...), branch_computations={%region_0.0_spmd, %region_1.2_spmd} | conditional | flops 3815386880 | bytes 37820160 | solution.py:344
  12.5 4.0 %convolution_convert_fusion.2 = bf16[512,768]{1,0:T(8,128)(2,1)} fusion(bf16[512,1152]{1,0:T(8,128)(2,1)} %get-tuple-element.34, bf16[512,1152]{1,0:T(8,128)(2,1)} %get-tuple-element.50, pred[]{:T(512)S(6)} %eq.14, s32[]{:T(128)S(6)} %mul.19, s32[768]{0:T(1024)S(1)} %get-tuple-element.121, s32[768]{0:T(1024)S(1)} %get-tuple-element.122, ...), kind=kOutput, calls=%fused_computation.40 | convolution fusion | flops 953843712 | bytes 3159557 | tf_op jit(solution)/shard_map/cond/branch_1_fun/dot_general | solution.py:353
  16.5 2.6 %convolution_convert_fusion = bf16[512,768]{1,0:T(8,128)(2,1)} fusion(bf16[512,1152]{1,0:T(8,128)(2,1)S(1)} %copy-done.5, bf16[512,1152]{1,0:T(8,128)(2,1)S(1)} %copy-done.3, pred[]{:T(512)S(6)} %eq.14, s32[]{:T(128)S(6)} %mul.19, s32[768]{0:T(1024)S(1)} %get-tuple-element.121, s32[768]{0:T(1024)S(1)} %get-tuple-element.122, ...), kind=kOutput, calls=%fused_computation.38 | convolution fusion | flops 953843712 | bytes 3159557 | tf_op jit(solution)/shard_map/cond/branch_1_fun/dot_general | solution.py:353
  19.6 4.0 %convolution_convert_fusion.1 = bf16[512,768]{1,0:T(8,128)(2,1)} fusion(bf16[512,1152]{1,0:T(8,128)(2,1)} %get-tuple-element.50, bf16[512,1152]{1,0:T(8,128)(2,1)} %get-tuple-element.34, pred[]{:T(512)S(6)} %eq.14, s32[]{:T(128)S(6)} %mul.16, s32[768]{0:T(1024)S(1)} %get-tuple-element.121, s32[768]{0:T(1024)S(1)} %get-tuple-element.122, ...), kind=kOutput, calls=%fused_computation.39 | convolution fusion | flops 953843712 | bytes 3159557 | tf_op jit(solution)/shard_map/cond/branch_1_fun/dot_general | solution.py:352
  23.6 1.8 %convolution_convert_fusion.3 = bf16[512,768]{1,0:T(8,128)(2,1)S(1)} fusion(bf16[512,1152]{1,0:T(8,128)(2,1)S(1)} %copy-done.4, bf16[512,1152]{1,0:T(8,128)(2,1)S(1)} %copy-done.6, pred[]{:T(512)S(6)} %eq.14, s32[]{:T(128)S(6)} %mul.16, s32[768]{0:T(1024)S(1)} %get-tuple-element.121, s32[768]{0:T(1024)S(1)} %get-tuple-element.122, ...), kind=kOutput, calls=%fused_computation.41 | convolution fusion | flops 953843712 | bytes 3159557 | tf_op jit(solution)/shard_map/cond/branch_1_fun/dot_general | solution.py:352
  25.4 4.5 %side_first.3 = f32[512,1152]{1,0:T(8,128)} custom-call(bf16[512,1152]{1,0:T(8,128)(2,1)S(1)} %get-tuple-element.52.refs_0_.refs_1_, bf16[512,1152]{1,0:T(8,128)(2,1)} %get-tuple-element.53.refs_1_.refs_0_), custom_call_target="tpu_custom_call" | custom-call | flops 1000 | bytes 1000 | tf_op jit(solution)/shard_map/cond/branch_1_fun/side_first/pallas_call | solution.py:174
  29.9 4.3 %side_first.4 = f32[512,1152]{1,0:T(8,128)} custom-call(bf16[512,1152]{1,0:T(8,128)(2,1)} %get-tuple-element.53.refs_1_.refs_0_, bf16[512,1152]{1,0:T(8,128)(2,1)S(1)} %get-tuple-element.52.refs_0_.refs_1_), custom_call_target="tpu_custom_call" | custom-call | flops 1000 | bytes 1000 | tf_op jit(solution)/shard_map/cond/branch_1_fun/side_first/pallas_call | solution.py:174
  34.2 3.3 %collective-permute-done.5.a_cross = bf16[512,1152]{1,0:T(8,128)(2,1)} collective-permute-done((bf16[512,1152]{1,0:T(8,128)(2,1)S(1)}, bf16[512,1152]{1,0:T(8,128)(2,1)}, u32[]{:S(2)}, u32[]{:S(2)}) %collective-permute-start.5) | collective-permute-done | bytes 1179680 | tf_op jit(solution)/shard_map/ppermute | solution.py:300
  39.5 13.3 %conditional.4 = (bf16[16,336,128]{2,1,0:T(8,128)(2,1)}) conditional(s32[]{:T(128)} %convert_element_type.19, () %tuple.39, (bf16[512,1152]{1,0:T(8,128)(2,1)S(1)}, bf16[512,1152]{1,0:T(8,128)(2,1)}, bf16[512,1152]{1,0:T(8,128)(2,1)}, f32[512,1152]{1,0:T(8,128)}, f32[512,1152]{1,0:T(8,128)}, /*index=5*/f32[512,1]{1,0:T(8,128)}, ...), branch_computations={%region_2.3_spmd, %region_3.4_spmd} | conditional | flops 3000 | bytes 4721640 | solution.py:344
  39.5 7.3 %side_last.2.grad = bf16[1152,512]{1,0:T(8,128)(2,1)S(1)} custom-call(bf16[512,1152]{1,0:T(8,128)(2,1)S(1)} %get-tuple-element.54.refs_0_, bf16[512,1152]{1,0:T(8,128)(2,1)} %get-tuple-element.55.refs_1_, bf16[512,1152]{1,0:T(8,128)(2,1)} %get-tuple-element.56.refs_2_, f32[512,1152]{1,0:T(8,128)} %get-tuple-element.57.refs_3_, ...), custom_call_target="tpu_custom_call" | custom-call | flops 1000 | bytes 1000 | tf_op jit(solution)/shard_map/cond/branch_1_fun/side_last/pallas_call | solution.py:174
  48.0 1.7 %collective-permute-done.grad = bf16[1152,512]{1,0:T(8,128)(2,1)S(1)} collective-permute-done((bf16[1152,512]{1,0:T(8,128)(2,1)S(1)}, bf16[1152,512]{1,0:T(8,128)(2,1)S(1)}, u32[]{:S(2)}, u32[]{:S(2)}) %collective-permute-start) | collective-permute-done | bytes 1179680 | tf_op jit(solution)/shard_map/cond/branch_1_fun/ppermute | solution.py:300
  49.7 3.1 %head_pack.2 = bf16[16,336,128]{2,1,0:T(8,128)(2,1)} custom-call(bf16[1152,512]{1,0:T(8,128)(2,1)S(1)} %collective-permute-done.grad, bf16[512,768]{1,0:T(8,128)(2,1)} %get-tuple-element.60.feats, f32[1152,768]{1,0:T(8,128)S(1)} %head_own.2.before), custom_call_target="tpu_custom_call" | custom-call | flops 1000 | bytes 1000 | tf_op jit(solution)/shard_map/cond/branch_1_fun/head_pack/pallas_call | solution.py:368
  52.8 6.0 %all-to-all-start = ((bf16[4,4,336,128]{3,2,1,0:T(8,128)(2,1)}), bf16[4,4,336,128]{3,2,1,0:T(8,128)(2,1)S(1)}, u32[]{:S(2)}, u32[]{:S(2)}) async-start(bf16[4,4,336,128]{3,2,1,0:T(8,128)(2,1)} %bitcast.3), calls=%async_computation | async-start | bytes 2752512 | tf_op jit(solution)/shard_map/all_to_all | solution.py:381
  58.8 4.5 %side_first.5 = f32[512,1152]{1,0:T(8,128)} custom-call(bf16[512,1152]{1,0:T(8,128)(2,1)} %get-tuple-element.97.refs_0_.b_emb, bf16[512,1152]{1,0:T(8,128)(2,1)S(1)} %collective-permute-done.7.refs_1_.a_from, f32[512,1152]{1,0:T(8,128)} %get-tuple-element.103.refs_2_), custom_call_target="tpu_custom_call" | custom-call | flops 1000 | bytes 1000 | tf_op jit(solution)/shard_map/side_first/pallas_call | solution.py:174
  64.7 10.6 %conditional.5 = (bf16[16,336,128]{2,1,0:T(8,128)(2,1)}) conditional(s32[]{:T(128)} %convert_element_type.19, () %tuple.34, (bf16[512,1152]{1,0:T(8,128)(2,1)}, bf16[512,1152]{1,0:T(8,128)(2,1)}, f32[512,1152]{1,0:T(8,128)}, f32[512,1152]{1,0:T(8,128)}, f32[512,1]{1,0:T(8,128)S(1)}, /*index=5*/bf16[512,768]{1,0:T(8,128)(2,1)}, ...), branch_computations={%region_4.5_spmd, %region_5.6_spmd} | conditional | flops 3000 | bytes 4721640 | solution.py:344
  64.7 4.6 %side_last.3.grad = bf16[1152,512]{1,0:T(8,128)(2,1)S(1)} custom-call(bf16[512,1152]{1,0:T(8,128)(2,1)} %get-tuple-element.62.refs_0_, bf16[512,1152]{1,0:T(8,128)(2,1)} %get-tuple-element.63.refs_1_, f32[512,1152]{1,0:T(8,128)} %get-tuple-element.64.refs_2_, f32[512,1152]{1,0:T(8,128)} %get-tuple-element.65.refs_3_, f32[512,1]{1,0:T(8,128)S(1)} %get-tuple-element.66.refs_4_), custom_call_target="tpu_custom_call" | custom-call | flops 1000 | bytes 1000 | tf_op jit(solution)/shard_map/cond/branch_1_fun/side_last/pallas_call | solution.py:174
  69.4 2.2 %head_own.3.before = f32[1152,768]{1,0:T(8,128)S(1)} custom-call(bf16[1152,512]{1,0:T(8,128)(2,1)S(1)} %side_last.3.grad, bf16[512,768]{1,0:T(8,128)(2,1)} %get-tuple-element.68.feats), custom_call_target="tpu_custom_call" | custom-call | flops 1000 | bytes 1000 | tf_op jit(solution)/shard_map/cond/branch_1_fun/head_own/pallas_call | solution.py:367
  72.2 3.1 %head_pack.3 = bf16[16,336,128]{2,1,0:T(8,128)(2,1)} custom-call(bf16[1152,512]{1,0:T(8,128)(2,1)S(1)} %collective-permute-done.1.grad, bf16[512,768]{1,0:T(8,128)(2,1)} %get-tuple-element.67.feats, f32[1152,768]{1,0:T(8,128)S(1)} %head_own.3.before), custom_call_target="tpu_custom_call" | custom-call | flops 1000 | bytes 1000 | tf_op jit(solution)/shard_map/cond/branch_1_fun/head_pack/pallas_call | solution.py:368
  76.2 8.3 %all-to-all-start.1 = ((bf16[16,336,128]{2,1,0:T(8,128)(2,1)}), bf16[16,336,128]{2,1,0:T(8,128)(2,1)S(1)}, u32[]{:S(2)}, u32[]{:S(2)}) async-start(bf16[16,336,128]{2,1,0:T(8,128)(2,1)} %get-tuple-element.139), calls=%async_computation.1 | async-start | bytes 2752512 | tf_op jit(solution)/shard_map/all_to_all | solution.py:393
  90.1 7.1 %loss.1 = f32[1,512]{1,0:T(1,128)} custom-call(s32[1]{0:T(128)} %bitcast.odd.use_a, bf16[512,1152]{1,0:T(8,128)(2,1)} %copy-done.2, bf16[512,1152]{1,0:T(8,128)(2,1)} %get-tuple-element.97.refs_0_.b_emb, bf16[512,1152]{1,0:T(8,128)(2,1)} %collective-permute-done.5.a_cross, bf16[512,1152]{1,0:T(8,128)(2,1)} %collective-permute-done.6.b_cross, ...), custom_call_target="tpu_custom_call" | custom-call | flops 1000 | bytes 1000 | tf_op jit(solution)/shard_map/loss/pallas_call | solution.py:396
  97.2 8.5 %all-to-all-done.1.b_got = bf16[16,336,128]{2,1,0:T(8,128)(2,1)S(1)} async-done(((bf16[16,336,128]{2,1,0:T(8,128)(2,1)}), bf16[16,336,128]{2,1,0:T(8,128)(2,1)S(1)}, u32[]{:S(2)}, u32[]{:S(2)}) %all-to-all-start.1) | async-done | bytes 1376288 | tf_op jit(solution)/shard_map/all_to_all | solution.py:393
  106.8 18.1 %all_to_all.15.got = bf16[8,2,48,128]{3,2,1,0:T(8,128)(2,1)S(1)} all-to-all(bf16[8,2,48,128]{3,2,1,0:T(8,128)(2,1)S(1)} %add_pack.1), channel_id=1, replica_groups=mesh['y'=4,'xlo'=2,'xhi'=2,'z'=8,'core'=2] {'z'}, dimensions={0} | all-to-all | bytes 393216 | tf_op jit(solution)/shard_map/all_to_all | solution.py:403
  (43 shorter events, 15.5 us)
Async XLA Ops:
  9.6 29.9 %copy-start.2 = (bf16[512,1152]{1,0:T(8,128)(2,1)}, bf16[512,1152]{1,0:T(8,128)(2,1)S(1)}, u32[]{:S(2)}) copy-start(bf16[512,1152]{1,0:T(8,128)(2,1)S(1)} %get-tuple-element.112.a_emb) | copy-start | bytes 3538948
  9.6 27.9 %collective-permute-start.5 = (bf16[512,1152]{1,0:T(8,128)(2,1)S(1)}, bf16[512,1152]{1,0:T(8,128)(2,1)}, u32[]{:S(2)}, u32[]{:S(2)}) collective-permute-start(bf16[512,1152]{1,0:T(8,128)(2,1)S(1)} %get-tuple-element.112.a_emb), channel_id=1, source_target_pairs={{0,32},{1,33},{2,34},{3,35},{4,36},{5,37},{6,38},{7,39},{8,40},{9,... | collective-permute-start | bytes 3538952 | tf_op jit(solution)/shard_map/ppermute | solution.py:300
  10.3 27.7 %collective-permute-start.4 = (bf16[512,1152]{1,0:T(8,128)(2,1)}, bf16[512,1152]{1,0:T(8,128)(2,1)}, u32[]{:S(2)}, u32[]{:S(2)}) collective-permute-start(bf16[512,1152]{1,0:T(8,128)(2,1)} %get-tuple-element.97.refs_0_.b_emb), channel_id=1, source_target_pairs={{0,192},{1,193},{2,194},{3,195},{4,196},{5,197},{6,198},{7,199},{8... | collective-permute-start | bytes 3538952 | tf_op jit(solution)/shard_map/ppermute | solution.py:300
  11.8 27.7 %collective-permute-start.7 = (bf16[512,1152]{1,0:T(8,128)(2,1)S(1)}, bf16[512,1152]{1,0:T(8,128)(2,1)S(1)}, u32[]{:S(2)}, u32[]{:S(2)}) collective-permute-start(bf16[512,1152]{1,0:T(8,128)(2,1)S(1)} %get-tuple-element.112.a_emb), channel_id=1, source_target_pairs={{0,64},{1,65},{2,66},{3,67},{4,68},{5,69},{6,70},{7,71},{8,72},{9,... | collective-permute-start | bytes 3538952 | tf_op jit(solution)/shard_map/ppermute | solution.py:300
  12.5 4.0 %copy-start.3 = (bf16[512,1152]{1,0:T(8,128)(2,1)S(1)}, bf16[512,1152]{1,0:T(8,128)(2,1)}, u32[]{:S(2)}) copy-start(bf16[512,1152]{1,0:T(8,128)(2,1)} %get-tuple-element.34) | copy-start | bytes 3538948 | tf_op jit(solution)/shard_map/cond
  12.5 4.0 %copy-start.5 = (bf16[512,1152]{1,0:T(8,128)(2,1)S(1)}, bf16[512,1152]{1,0:T(8,128)(2,1)}, u32[]{:S(2)}) copy-start(bf16[512,1152]{1,0:T(8,128)(2,1)} %get-tuple-element.50) | copy-start | bytes 3538948 | tf_op jit(solution)/shard_map/cond
  16.5 17.7 %collective-permute-start.2 = (bf16[512,768]{1,0:T(8,128)(2,1)}, bf16[512,768]{1,0:T(8,128)(2,1)}, u32[]{:S(2)}, u32[]{:S(2)}) collective-permute-start(bf16[512,768]{1,0:T(8,128)(2,1)} %convolution_convert_fusion.2), channel_id=1, source_target_pairs={{0,1},{1,0},{2,3},{3,2},{4,5},{5,4},{6,7},{7,6},{8,9},{9,8},{10,11... | collective-permute-start | bytes 2359304 | tf_op jit(solution)/shard_map/cond/branch_1_fun/ppermute | solution.py:300
  19.1 15.2 %collective-permute-start.3 = (bf16[512,768]{1,0:T(8,128)(2,1)}, bf16[512,768]{1,0:T(8,128)(2,1)}, u32[]{:S(2)}, u32[]{:S(2)}) collective-permute-start(bf16[512,768]{1,0:T(8,128)(2,1)} %convolution_convert_fusion), channel_id=1, source_target_pairs={{0,1},{1,0},{2,3},{3,2},{4,5},{5,4},{6,7},{7,6},{8,9},{9,8},{10,11... | collective-permute-start | bytes 2359304 | tf_op jit(solution)/shard_map/cond/branch_1_fun/ppermute | solution.py:300
  19.6 4.0 %copy-start.4 = (bf16[512,1152]{1,0:T(8,128)(2,1)S(1)}, bf16[512,1152]{1,0:T(8,128)(2,1)}, u32[]{:S(2)}) copy-start(bf16[512,1152]{1,0:T(8,128)(2,1)} %get-tuple-element.34) | copy-start | bytes 3538948 | tf_op jit(solution)/shard_map/cond
  19.6 4.0 %copy-start.6 = (bf16[512,1152]{1,0:T(8,128)(2,1)S(1)}, bf16[512,1152]{1,0:T(8,128)(2,1)}, u32[]{:S(2)}) copy-start(bf16[512,1152]{1,0:T(8,128)(2,1)} %get-tuple-element.50) | copy-start | bytes 3538948 | tf_op jit(solution)/shard_map/cond
  38.0 26.7 %collective-permute-start.6 = (bf16[512,1152]{1,0:T(8,128)(2,1)}, bf16[512,1152]{1,0:T(8,128)(2,1)}, u32[]{:S(2)}, u32[]{:S(2)}) collective-permute-start(bf16[512,1152]{1,0:T(8,128)(2,1)} %collective-permute-done.4.b_from), channel_id=1, source_target_pairs={{0,32},{1,33},{2,34},{3,35},{4,36},{5,37},{6,38},{7,39},{8,40},{9,... | collective-permute-start | bytes 3538952 | tf_op jit(solution)/shard_map/ppermute | solution.py:300
  39.5 19.3 %copy-start = (bf16[512,1152]{1,0:T(8,128)(2,1)}, bf16[512,1152]{1,0:T(8,128)(2,1)S(1)}, u32[]{:S(2)}) copy-start(bf16[512,1152]{1,0:T(8,128)(2,1)S(1)} %collective-permute-done.7.refs_1_.a_from) | copy-start | bytes 3538948
  46.8 2.9 %collective-permute-start = (bf16[1152,512]{1,0:T(8,128)(2,1)S(1)}, bf16[1152,512]{1,0:T(8,128)(2,1)S(1)}, u32[]{:S(2)}, u32[]{:S(2)}) collective-permute-start(bf16[1152,512]{1,0:T(8,128)(2,1)S(1)} %side_last.2.grad), channel_id=1, source_target_pairs={{0,1},{1,0},{2,3},{3,2},{4,5},{5,4},{6,7},{7,6},{8,9},{9,8},{10,11... | collective-permute-start | bytes 3538952 | tf_op jit(solution)/shard_map/cond/branch_1_fun/ppermute | solution.py:300
  52.8 23.4 %all-to-all-start = ((bf16[4,4,336,128]{3,2,1,0:T(8,128)(2,1)}), bf16[4,4,336,128]{3,2,1,0:T(8,128)(2,1)S(1)}, u32[]{:S(2)}, u32[]{:S(2)}) async-start(bf16[4,4,336,128]{3,2,1,0:T(8,128)(2,1)} %bitcast.3), calls=%async_computation | async-start | bytes 2752512 | tf_op jit(solution)/shard_map/all_to_all | solution.py:381
  58.8 5.9 %copy-start.7 = (f32[512,1]{1,0:T(8,128)S(1)}, f32[512,1]{1,0:T(8,128)}, u32[]{:S(2)}) copy-start(f32[512,1]{1,0:T(8,128)} %get-tuple-element.111) | copy-start | bytes 6148
  69.3 2.9 %collective-permute-start.1 = (bf16[1152,512]{1,0:T(8,128)(2,1)S(1)}, bf16[1152,512]{1,0:T(8,128)(2,1)S(1)}, u32[]{:S(2)}, u32[]{:S(2)}) collective-permute-start(bf16[1152,512]{1,0:T(8,128)(2,1)S(1)} %side_last.3.grad), channel_id=1, source_target_pairs={{0,1},{1,0},{2,3},{3,2},{4,5},{5,4},{6,7},{7,6},{8,9},{9,8},{10,11... | collective-permute-start | bytes 3538952 | tf_op jit(solution)/shard_map/cond/branch_1_fun/ppermute | solution.py:300
  76.2 29.5 %all-to-all-start.1 = ((bf16[16,336,128]{2,1,0:T(8,128)(2,1)}), bf16[16,336,128]{2,1,0:T(8,128)(2,1)S(1)}, u32[]{:S(2)}, u32[]{:S(2)}) async-start(bf16[16,336,128]{2,1,0:T(8,128)(2,1)} %get-tuple-element.139), calls=%async_computation.1 | async-start | bytes 2752512 | tf_op jit(solution)/shard_map/all_to_all | solution.py:393
  84.7 21.0 %collective-permute-start.10 = (bf16[336,128]{1,0:T(8,128)(2,1)S(1)}, bf16[336,128]{1,0:T(8,128)(2,1)S(1)}, u32[]{:S(2)}, u32[]{:S(2)}) collective-permute-start(bf16[336,128]{1,0:T(8,128)(2,1)S(1)} %get-tuple-element.116), channel_id=1, source_target_pairs={{0,48},{1,49},{2,50},{3,51},{4,52},{5,53},{6,54},{7,55},{8,56},{9,... | collective-permute-start | bytes 258056 | tf_op jit(solution)/shard_map/ppermute | solution.py:300
  86.2 20.1 %collective-permute-start.8 = (bf16[336,128]{1,0:T(8,128)(2,1)S(1)}, bf16[336,128]{1,0:T(8,128)(2,1)S(1)}, u32[]{:S(2)}, u32[]{:S(2)}) collective-permute-start(bf16[336,128]{1,0:T(8,128)(2,1)S(1)} %get-tuple-element.114), channel_id=1, source_target_pairs={{0,16},{1,17},{2,18},{3,19},{4,20},{5,21},{6,22},{7,23},{8,24},{9,... | collective-permute-start | bytes 258056 | tf_op jit(solution)/shard_map/ppermute | solution.py:300
  87.4 18.9 %collective-permute-start.9 = (bf16[336,128]{1,0:T(8,128)(2,1)S(1)}, bf16[336,128]{1,0:T(8,128)(2,1)S(1)}, u32[]{:S(2)}, u32[]{:S(2)}) collective-permute-start(bf16[336,128]{1,0:T(8,128)(2,1)S(1)} %get-tuple-element.115), channel_id=1, source_target_pairs={{0,32},{1,33},{2,34},{3,35},{4,36},{5,37},{6,38},{7,39},{8,40},{9,... | collective-permute-start | bytes 258056 | tf_op jit(solution)/shard_map/ppermute | solution.py:300
  88.9 1.3 %copy-start.1 = (bf16[512,1152]{1,0:T(8,128)(2,1)S(1)}, bf16[512,1152]{1,0:T(8,128)(2,1)}, u32[]{:S(2)}) copy-start(bf16[512,1152]{1,0:T(8,128)(2,1)} %copy-done) | copy-start | bytes 3538948
